TPU v7x, 256 devices: a whole 4x4x8 slice. The times are simulated.
256 devices in a mesh: samp: 32 (over x, z_hi, y), par: 8 (over z_lo, core).
Axes of the slice: x: 4, y: 4, z: 8 (z_hi: 2, z_lo: 4; z = z_hi * 4 + z_lo), core: 2. Of those that a mesh axis runs over, the one named last changes fastest.
Arguments:
- spins: int32 [256, 100], P('samp'), may hold values from -1 to 1, as said below
- embed: float32 [4, 64], replicated, may hold values from -3 to 3
- position: float32 [25, 64], replicated, may hold values from -3 to 3
- w_first: bfloat16 [64, 256], P(None, 'par'), may hold values from -0.75 to 0.75
- bias_first: float32 [256], P('par'), may hold values from -3 to 3
- readout: float32 [256], P('par'), may hold values from -1.2 to 1.2
- other_grads: bfloat16 [256, 32768], P('samp', 'par'), may hold values from -3 to 3
- energies: float32 [256], replicated, may hold values from -6 to 6
- shift: float32 [1], replicated, may hold values from 0.5 to 2
Outputs:
- coeffs: float32 [256], P('samp')
- update: float32 [64, 256], P(None, 'par')
- update_rest: float32 [32768], P('par')
Inputs may be any that keep to these rules, and one draw needn't show every extreme that they name: `spins`: every entry is -1 or +1.
All inputs are finite; a program needn't handle non-finite values.
Results may differ from a plain program's by a relative error of at most 0.0054.
The roundings to bfloat16 on the way count: a program that leaves them out, or rounds other values in their place, can miss the bound.
Values may be sent and summed in bfloat16 or wider, within the bound.
A program may use at most 64 MiB of HBM per device.

v0:
```python
import math

import jax
import jax.numpy as jnp
from jax import lax
from jax.sharding import PartitionSpec as P

LSIDE = 10
PATCH = 2
PATCHES = 25
PDIM = 4


def embed_rows(spins, embed, position):
    count = spins.shape[0]
    sides = LSIDE // PATCH
    blocks = spins.reshape(count, sides, PATCH, sides, PATCH).transpose(0, 1, 3, 2, 4)
    patches = blocks.reshape(count, PATCHES, PDIM).astype(jnp.float32)
    return (
        jnp.einsum("spk,kd->spd", patches, embed, precision=lax.Precision.HIGHEST) + position
    ).astype(jnp.bfloat16)


def derivatives(hidden, w_first, bias_first, readout):
    count = hidden.shape[0]
    act = (
        jnp.einsum("spd,df->spf", hidden, w_first, preferred_element_type=jnp.float32) + bias_first
    )
    slope = readout * jnp.tanh(act)
    grads = jnp.einsum(
        "spd,spf->sdf", hidden.astype(jnp.float32), slope, precision=lax.Precision.HIGHEST
    )
    return grads.reshape(count, hidden.shape[2] * w_first.shape[1])


def per_device(spins, embed, position, w_first, bias_first, readout, other_grads, energies, shift):
    own_count = spins.shape[0]
    total_count = energies.shape[0]
    layer_width = embed.shape[1] * w_first.shape[1]
    scale = 1.0 / math.sqrt(total_count)
    first_row = lax.axis_index("samp") * own_count
    hidden = embed_rows(spins, embed, position)
    own = derivatives(hidden, w_first, bias_first, readout)
    layer_sums, other_sums = lax.psum(
        (jnp.sum(own, axis=0), jnp.sum(other_grads, axis=0, dtype=jnp.float32)), "samp"
    )
    centered_layer = ((own - layer_sums / total_count) * scale).astype(jnp.bfloat16)
    centered_other = ((other_grads - other_sums / total_count) * scale).astype(jnp.bfloat16)
    centered = jnp.concatenate([centered_layer, centered_other], axis=1)
    block = lax.dot_general(
        centered,
        lax.all_gather(centered, "samp", axis=0, tiled=True),
        (((1,), (1,)), ((), ())),
        preferred_element_type=jnp.float32,
    )
    summed = lax.psum(block, "par")
    gram = lax.all_gather(summed, "samp", axis=0, tiled=True)
    matrix = gram + shift[0] * jnp.eye(total_count, dtype=jnp.float32)
    lower = jnp.linalg.cholesky(matrix)
    target = energies - jnp.sum(energies) / total_count
    solved = jax.scipy.linalg.cho_solve((lower, True), target)
    coeffs = lax.dynamic_slice_in_dim(solved, first_row, own_count, 0)
    partial_update = jnp.dot(coeffs, centered.astype(jnp.float32), precision=lax.Precision.HIGHEST)
    full = lax.psum(partial_update, "samp")
    update = full[:layer_width].reshape(embed.shape[1], w_first.shape[1])
    return (coeffs, update, full[layer_width:])


def solution(mesh):
    return jax.shard_map(
        per_device,
        mesh=mesh,
        in_specs=(
            P("samp", None),
            P(),
            P(),
            P(None, "par"),
            P("par"),
            P("par"),
            P("samp", "par"),
            P(),
            P(),
        ),
        out_specs=(P("samp"), P(None, "par"), P("par")),
        check_vma=False,
    )
```

profile of v0, /device:TPU:0, one launch (start us, length us, event | category | flops | bytes accessed | tf_op | source)
XLA Modules:
  0.0 744.1 jit_solution(15212910457913260659)
XLA Ops:
  7.2 0.7 convert_element_type.28
  8.2 1.1 fusion.2
  9.4 0.8 fusion.1
  10.6 0.9 convert_reduce_fusion
  11.5 224.7 %all-reduce.1 = (f32[4096]{0:T(1024)S(1)}, f32[2048]{0:T(1024)S(1)}) all-reduce(f32[4096]{0:T(1024)S(1)} %convert_reduce_fusion, f32[2048]{0:T(1024)S(1)} %reduce_sum.30), channel_id=1, replica_groups=mesh['samp'=32,'par'=8] {'samp'}, use_global_device_ids=true, to_apply=%region_3.0 | all-reduce | flops 6144 | bytes 49152 | tf_op jit(solution)/shard_map/psum | solution.py:44
  236.5 0.9 fusion.9
  237.4 0.6 pad_maximum_fusion
  238.7 1.3 reduce_sum.32
  240.7 0.7 broadcast_subtract_fusion
  241.3 90.7 %all-gather.2.cloned.1.call-done = bf16[256,6144]{1,0:T(8,128)(2,1)} async-done(((bf16[8,6144]{1,0:T(8,128)(2,1)}), bf16[256,6144]{1,0:T(8,128)(2,1)}) %all-gather.2.cloned.1.call-update) | async-done | bytes 3145744 | tf_op jit(solution)/shard_map/all_gather | solution.py:52
  332.1 2.9 fusion.24
  334.9 13.9 %psum.30 = f32[8,256]{1,0:T(8,128)S(1)} all-reduce(f32[8,256]{1,0:T(8,128)S(1)} %fusion.24), channel_id=1, replica_groups=mesh['samp'=32,'par'=8] {'par'}, use_global_device_ids=true, to_apply=%region_4.0 | all-reduce | flops 2048 | bytes 16384 | tf_op jit(solution)/shard_map/psum | solution.py:56
  348.9 109.8 %all_gather.7 = f32[256,256]{1,0:T(8,128)S(1)} all-gather(f32[8,256]{1,0:T(8,128)S(1)} %psum.30), channel_id=1, replica_groups=mesh['samp'=32,'par'=8] {'samp'}, dimensions={0}, use_global_device_ids=true | all-gather | bytes 270336 | tf_op jit(solution)/shard_map/all_gather | solution.py:57
  459.0 11.7 %cholesky.49 = f32[128,128]{1,0:T(8,128)S(1)} custom-call(f32[128,128]{1,0:T(8,128)S(1)} %cholesky.115), custom_call_target="Cholesky" | custom-call | tf_op jit(solution)/shard_map/jit(cholesky)/cholesky | solution.py:59
  470.7 9.8 %custom-call.18 = f32[1,128,128]{1,2,0:T(8,128)S(1)} custom-call(f32[1,128,128]{2,1,0:T(8,128)S(1)} %get-tuple-element.42), custom_call_target="InvertDiagBlocksLowerTriangular" | custom-call | tf_op jit(solution)/shard_map/jit(cholesky)/cholesky | solution.py:59
  481.0 11.7 %cholesky.103 = f32[128,128]{1,0:T(8,128)S(1)} custom-call(f32[128,128]{1,0:T(8,128)S(1)} %convolution_subtract_fusion), custom_call_target="Cholesky" | custom-call | tf_op jit(solution)/shard_map/jit(cholesky)/cholesky | solution.py:59
  493.1 0.6 compare_reduce_fusion
  495.2 4.4 while.1
  496.0 1.4 dynamic-slice.8
  498.1 1.4 dynamic-slice.8
  499.6 19.7 %custom-call.19 = f32[2,128,128]{1,2,0:T(8,128)S(1)} custom-call(f32[2,128,128]{2,1,0:T(8,128)S(1)} %get-tuple-element.10), custom_call_target="InvertDiagBlocksLowerTriangular" | custom-call | tf_op jit(solution)/shard_map/jit(_cho_solve)/triangular_solve | solution.py:61
  520.8 215.0 %psum.31 = f32[6144]{0:T(1024)S(1)} all-reduce(f32[6144]{0:T(1024)S(1)} %bitcast.92), channel_id=1, replica_groups=mesh['samp'=32,'par'=8] {'samp'}, use_global_device_ids=true, to_apply=%region_10.11 | all-reduce | flops 6144 | bytes 49152 | tf_op jit(solution)/shard_map/psum | solution.py:64
  735.8 0.6 slice.92
  736.5 0.7 copy.42
  (57 shorter events, 5.3 us)
Async XLA Ops:
  7.2 2.2 copy-start
  7.2 324.9 %all-gather.2.cloned.1.call-start = ((), (), s32[]{:S(2)}) async-start(), calls=%async_computation | async-start | bytes 3244032 | tf_op jit(solution)/shard_map/all_gather | solution.py:52
  458.8 61.8 %copy-start.1 = (bf16[8,6144]{1,0:T(8,128)(2,1)S(1)}, bf16[8,6144]{1,0:T(8,128)(2,1)}, u32[]{:S(2)}) copy-start(bf16[8,6144]{1,0:T(8,128)(2,1)} %pad_maximum_fusion) | copy-start | bytes 294916
  520.6 216.7 %copy-start.2 = (f32[8,1]{0,1:T(1,128)}, f32[8,1]{0,1:T(1,128)S(1)}, u32[]{:S(2)}) copy-start(f32[8,1]{0,1:T(1,128)S(1)} %fusion.18) | copy-start | bytes 100
Sparse Core Ops, SparseCore 0:
  238.2 93.8 all-gather.1
where the time goes:
time: 745 us; the launch traced here: 744 us
  blocking collectives  563 us (76%)
  waiting for transfers between devices  90.7 us (12%)
  other arithmetic  58.9 us (8%)
  between operations  16.9 us (2%)
    psum x1, blocking collectives, per_device(): lax.psum((jnp.sum(own, axis=0), jnp.sum(other_grads, axis=0, dtype=jnp.fl...  225 us
    psum x1, blocking collectives, per_device(): full = lax.psum(partial_update, 'samp')  215 us
    all_gather x1, blocking collectives, per_device(): gram = lax.all_gather(summed, 'samp', axis=0, tiled=True)  110 us
    all_gather x1, waiting for transfers between devices, per_device(): lax.all_gather(centered, 'samp', axis=0, tiled=True)  90.7 us
    another operation x6, other arithmetic, per_device(): lower = jnp.linalg.cholesky(matrix)  33.9 us
    another operation x4, other arithmetic, per_device(): solved = jax.scipy.linalg.cho_solve((lower, True), target)  19.8 us
  transfers between devices with their start and end apart: 1, of which 1 were waited for; matrix products, arithmetic and copies ran while one was open for 0% of the time, Pallas kernels for 0%

commit v1 on v0

v1 whole, which is shorter than its diff:
```python
import functools

import jax
import jax.numpy as jnp
from jax import lax
from jax.experimental import pallas as pl
from jax.experimental.pallas import tpu as pltpu
from jax.sharding import PartitionSpec as P

MESH = pl.DeviceIdType.MESH
HI = lax.Precision.HIGHEST
F32 = jnp.float32
BF16 = jnp.bfloat16

LSIDE = 10
PATCHES = 25
D = 64
SAMPLES = 256
OWN = 8
FOWN = 32
NSAMP = 32
NPAR = 8
NX, NZH, NY = 4, 2, 4
ROWS = PATCHES * OWN


def place():
    samp = lax.axis_index("samp")
    par = lax.axis_index("par")
    x, zh, y = samp // 8, (samp // 4) % 2, samp % 4
    zl, core = par // 2, par % 2
    return samp, par, x, zh, y, zl, core


def local_derivatives(spins_ref, embed_ref, position_ref, w_ref, bias_ref, readout_ref, spin_pad, table, w_pad, slope_pad):
    spin_pad[...] = jnp.zeros_like(spin_pad)
    spin_pad[:, 0:100] = spins_ref[...].astype(F32)
    table[0:4, 0:D] = embed_ref[...]
    table[0:4, D : 2 * D] = embed_ref[...]
    table[8 : 8 + PATCHES, 0:D] = position_ref[...]
    table[8 : 8 + PATCHES, D : 2 * D] = position_ref[...]
    site = lax.broadcasted_iota(jnp.int32, (128, 128), 0)
    line = (site * 205) >> 11
    kind = (line & 1) * 2 + ((site - line * 10) & 1)
    spread = jnp.where(
        kind == 0,
        table[0:1, :],
        jnp.where(kind == 1, table[1:2, :], jnp.where(kind == 2, table[2:3, :], table[3:4, :])),
    )
    site = lax.broadcasted_iota(jnp.int32, (ROWS, 128), 1)
    line = (site * 205) >> 11
    patch = (line >> 1) * 5 + ((site - line * 10) >> 1)
    row_patch = lax.broadcasted_iota(jnp.int32, (ROWS, 128), 0) >> 3
    own_spins = jnp.concatenate([spin_pad[...]] * PATCHES, axis=0)
    picked = jnp.where(patch == row_patch, own_spins, 0.0)
    offsets = jnp.concatenate(
        [jnp.broadcast_to(table[8 + p : 9 + p, :], (OWN, 128)) for p in range(PATCHES)], axis=0
    )
    hidden = (jnp.dot(picked, spread, precision=HI, preferred_element_type=F32) + offsets).astype(BF16)
    w_pad[...] = jnp.zeros_like(w_pad)
    w_pad[0:D, :] = w_ref[...].astype(F32)
    act = jnp.dot(hidden, w_pad[...].astype(BF16), preferred_element_type=F32) + bias_ref[...]
    slope_pad[...] = jnp.zeros_like(slope_pad)
    slope_pad[0:ROWS, 0:FOWN] = readout_ref[...] * jnp.tanh(act)
    slope_t = jnp.transpose(slope_pad[...])[0:FOWN, :]
    sample = lax.broadcasted_iota(jnp.int32, (OWN, 256), 0)
    row_sample = lax.broadcasted_iota(jnp.int32, (OWN, 256), 1) & 7
    same = (sample == row_sample)[None]
    left = jnp.where(same, jnp.broadcast_to(slope_t[:, None, :], (FOWN, OWN, 256)), 0.0)
    left = left.reshape(FOWN * OWN, 256)
    right = jnp.concatenate([hidden.astype(F32), jnp.zeros((256 - ROWS, 128), F32)], axis=0)
    return jnp.dot(left, right, precision=HI, preferred_element_type=F32)


def gram_kernel(
    spins_ref, embed_ref, position_ref, w_ref, bias_ref, readout_ref, other_ref,
    gram_ref, cent_ref,
    spin_pad, table, w_pad, slope_pad, sbuf, rbuf, cbuf, pair_out, pair_in, half, xy_in, z_in, send_sem, recv_sem,
):
    samp, par, x, zh, y, zl, core = place()
    q = x * 4 + y
    z = zh * 4 + zl
    mate = zl * 2 + (1 - core)

    def samp_peer(k):
        return (lax.rem(samp + k, NSAMP), par)

    def xy_peer(k):
        nx = lax.rem(x + k // 4, 4)
        ny = lax.rem(y + k % 4, 4)
        return nx * 4 + ny, (nx * 8 + zh * 4 + ny, par)

    def z_peer(k):
        nz = lax.rem(z + k, 8)
        return nz, (x * 8 + (nz // 4) * 4 + y, (nz % 4) * 2 + core)

    barrier = pltpu.get_barrier_semaphore()
    greeted = 0
    for k in range(1, NSAMP):
        pl.semaphore_signal(barrier, inc=1, device_id=samp_peer(k), device_id_type=MESH)
        greeted += 1
    for k in (1, 2, 3, 5, 6, 7):
        pl.semaphore_signal(barrier, inc=1, device_id=z_peer(k)[1], device_id_type=MESH)
        greeted += 1
    pl.semaphore_signal(barrier, inc=1, device_id=(samp, mate), device_id_type=MESH)
    greeted += 1

    grads = local_derivatives(
        spins_ref, embed_ref, position_ref, w_ref, bias_ref, readout_ref, spin_pad, table, w_pad, slope_pad
    )
    lane = lax.broadcasted_iota(jnp.int32, (256, 128), 1)
    high = grads.astype(BF16).astype(F32)
    terms = jnp.where(lane < D, high, grads - high)
    for j in range(NSAMP):
        sbuf[j] = jnp.concatenate(
            [other_ref[:, 128 * j : 128 * (j + 1)].astype(F32), terms[8 * j : 8 * (j + 1), :]], axis=0
        ).astype(BF16)

    pl.semaphore_wait(barrier, greeted)

    for k in range(1, NSAMP):
        to = samp_peer(k)
        pltpu.make_async_remote_copy(
            src_ref=sbuf.at[to[0]], dst_ref=rbuf.at[samp], send_sem=send_sem.at[0], recv_sem=recv_sem.at[0],
            device_id=to, device_id_type=MESH,
        ).start()
    rbuf[samp] = sbuf[samp]
    most = rbuf.at[pl.ds(0, NSAMP - 1)]
    pltpu.make_async_copy(most, most, recv_sem.at[0]).wait()

    got = rbuf[...].astype(F32)
    others = got[:, 0:8, :].reshape(SAMPLES, 128)
    pair = got[:, 8:16, :].reshape(SAMPLES, 128)
    layer = jnp.where(lane < D, pair + pltpu.roll(pair, D, 1), 0.0)
    for n, joined in enumerate((others, layer)):
        mean = jnp.sum(joined, axis=0, keepdims=True) / SAMPLES
        cbuf[:, 128 * n : 128 * (n + 1)] = ((joined - mean) * 0.0625).astype(BF16)
    cent_ref[...] = cbuf[...]

    def rows_of(c):
        return lax.dot_general(
            cbuf[pl.ds(pl.multiple_of(c * 128, 128), 128), :], cbuf[...], (((1,), (1,)), ((), ())),
            preferred_element_type=F32,
        )

    pair_out[...] = rows_of(1 - core)
    swap = pltpu.make_async_remote_copy(
        src_ref=pair_out, dst_ref=pair_in, send_sem=send_sem.at[1], recv_sem=recv_sem.at[1],
        device_id=(samp, mate), device_id_type=MESH,
    )
    swap.start()
    own = rows_of(core)
    swap.wait_recv()
    half[...] = (own + pair_in[...]).reshape(16, 8, 256)

    for k in range(1, 16):
        nq, to = xy_peer(k)
        pltpu.make_async_remote_copy(
            src_ref=half.at[nq], dst_ref=xy_in.at[q], send_sem=send_sem.at[2], recv_sem=recv_sem.at[2],
            device_id=to, device_id_type=MESH,
        ).start()
    xy_in[q] = half[q]
    most = xy_in.at[pl.ds(0, 15)]
    pltpu.make_async_copy(most, most, recv_sem.at[2]).wait()
    z_in[z] = jnp.sum(xy_in[...], axis=0)

    for k in range(1, 8):
        to = z_peer(k)[1]
        pltpu.make_async_remote_copy(
            src_ref=z_in.at[z], dst_ref=z_in.at[z], send_sem=send_sem.at[3], recv_sem=recv_sem.at[3],
            device_id=to, device_id_type=MESH,
        ).start()
    most = z_in.at[pl.ds(0, 7)]
    pltpu.make_async_copy(most, most, recv_sem.at[3]).wait()
    mine = core * 16 + q
    gram_ref[mine] = jnp.sum(z_in[...], axis=0)

    for k in range(1, 16):
        to = xy_peer(k)[1]
        pltpu.make_async_remote_copy(
            src_ref=gram_ref.at[mine], dst_ref=gram_ref.at[mine], send_sem=send_sem.at[4], recv_sem=recv_sem.at[4],
            device_id=to, device_id_type=MESH,
        ).start()
    most = gram_ref.at[pl.ds(core * 16, 15)]
    pltpu.make_async_copy(most, most, recv_sem.at[4]).wait()
    own_half = gram_ref.at[pl.ds(core * 16, 16)]
    swap = pltpu.make_async_remote_copy(
        src_ref=own_half, dst_ref=own_half, send_sem=send_sem.at[5], recv_sem=recv_sem.at[5],
        device_id=(samp, mate), device_id_type=MESH,
    )
    swap.start()
    swap.wait_recv()

    for ref, n, size in ((sbuf, 0, 31), (pair_out, 1, None), (half, 2, 15), (z_in, 3, 7), (gram_ref, 4, 15), (gram_ref, 5, 16)):
        part = ref if size is None else ref.at[pl.ds(0, size)]
        pltpu.make_async_copy(part, part, send_sem.at[n]).wait()


def gather_kernel(row_ref, rest_ref, layer_ref, recv, send_sem, recv_sem):
    samp, par = lax.axis_index("samp"), lax.axis_index("par")
    barrier = pltpu.get_barrier_semaphore()
    for k in range(1, NSAMP):
        pl.semaphore_signal(barrier, inc=1, device_id=(lax.rem(samp + k, NSAMP), par), device_id_type=MESH)
    recv[samp] = row_ref[...]
    pl.semaphore_wait(barrier, NSAMP - 1)
    for k in range(1, NSAMP):
        pltpu.make_async_remote_copy(
            src_ref=row_ref, dst_ref=recv.at[samp], send_sem=send_sem, recv_sem=recv_sem,
            device_id=(lax.rem(samp + k, NSAMP), par), device_id_type=MESH,
        ).start()
    most = recv.at[pl.ds(0, NSAMP - 1)]
    pltpu.make_async_copy(most, most, recv_sem).wait()
    got = recv[...]
    rest_ref[...] = got[:, 0, :]
    layer_ref[...] = jnp.transpose(got[:, 1, :])[0:D, :]
    pltpu.make_async_copy(most, most, send_sem).wait()


def per_device(spins, embed, position, w_first, bias_first, readout, other_grads, energies, shift):
    vmem = pl.BlockSpec(memory_space=pltpu.VMEM)
    gram, cent = pl.pallas_call(
        gram_kernel,
        out_shape=(jax.ShapeDtypeStruct((32, 8, 256), F32), jax.ShapeDtypeStruct((256, 256), BF16)),
        in_specs=[vmem] * 7,
        out_specs=(vmem, vmem),
        scratch_shapes=[
            pltpu.VMEM((8, 128), F32),
            pltpu.VMEM((40, 128), F32),
            pltpu.VMEM((128, FOWN), F32),
            pltpu.VMEM((256, 128), F32),
            pltpu.VMEM((NSAMP, 16, 128), BF16),
            pltpu.VMEM((NSAMP, 16, 128), BF16),
            pltpu.VMEM((256, 256), BF16),
            pltpu.VMEM((128, 256), F32),
            pltpu.VMEM((128, 256), F32),
            pltpu.VMEM((16, 8, 256), F32),
            pltpu.VMEM((16, 8, 256), F32),
            pltpu.VMEM((8, 8, 256), F32),
            pltpu.SemaphoreType.DMA((6,)),
            pltpu.SemaphoreType.DMA((6,)),
        ],
        compiler_params=pltpu.CompilerParams(
            collective_id=0, has_side_effects=True, vmem_limit_bytes=32 * 2**20
        ),
        name="gram",
    )(spins, embed, position, w_first, bias_first.reshape(1, -1), readout.reshape(1, -1), other_grads)
    matrix = gram.reshape(SAMPLES, SAMPLES) + shift[0] * jnp.eye(SAMPLES, dtype=F32)
    lower = jnp.linalg.cholesky(matrix)
    target = energies - jnp.sum(energies) / SAMPLES
    solved = jax.scipy.linalg.cho_solve((lower, True), target)
    coeffs = lax.dynamic_slice_in_dim(solved, lax.axis_index("samp") * OWN, OWN, 0)
    row = jnp.dot(solved, cent.astype(F32), precision=HI).reshape(2, 128)
    rest, layer = pl.pallas_call(
        gather_kernel,
        out_shape=(jax.ShapeDtypeStruct((NSAMP, 128), F32), jax.ShapeDtypeStruct((D, FOWN), F32)),
        in_specs=[vmem],
        out_specs=(vmem, vmem),
        scratch_shapes=[
            pltpu.VMEM((NSAMP, 2, 128), F32),
            pltpu.SemaphoreType.DMA,
            pltpu.SemaphoreType.DMA,
        ],
        compiler_params=pltpu.CompilerParams(
            collective_id=1, has_side_effects=True, vmem_limit_bytes=32 * 2**20
        ),
        name="gather",
    )(row)
    return (coeffs, layer, rest.reshape(-1))


def solution(mesh):
    return jax.shard_map(
        per_device,
        mesh=mesh,
        in_specs=(
            P("samp", None), P(), P(), P(None, "par"), P("par"), P("par"), P("samp", "par"), P(), P(),
        ),
        out_specs=(P("samp"), P(None, "par"), P("par")),
        check_vma=False,
    )
```

time: 745 us -> 119 us (0.16)
  the two profiles are of different devices: /device:TPU:0 before, /device:TPU:1 now
where the time goes in v1:
time: 119 us; the launch traced here: 118 us
  other arithmetic  55.1 us (46%)
  Pallas kernels  49.5 us (42%)
  local copies, waits for them, and re-layouts  8.39 us (7%)
  between operations  3.48 us (3%)
  matrix products  1.79 us (2%)
    pallas_call x1, Pallas kernels, per_device(): pl.pallas_call(gram_kernel, out_shape=(jax.ShapeDtypeStruct((32, 8, 256),...  37.9 us
    another operation x6, other arithmetic, per_device(): lower = jnp.linalg.cholesky(matrix)  34.1 us
    another operation x3, other arithmetic, per_device(): solved = jax.scipy.linalg.cho_solve((lower, True), target)  19.7 us
    pallas_call x1, Pallas kernels, per_device(): pl.pallas_call(gather_kernel, out_shape=(jax.ShapeDtypeStruct((NSAMP, 128...  11.6 us
    another operation x10, local copies, waits for them, and re-layouts  4.15 us
    unnamed x17, local copies, waits for them, and re-layouts  3.59 us

profile of v1, /device:TPU:1, one launch (start us, length us, event | category | flops | bytes accessed | tf_op | source)
XLA Modules:
  0.0 118.3 jit_solution(16166865978352998161)
XLA Ops:
  0.7 0.8 copy.20.w_ref
  1.5 0.6 copy-done.3
  2.1 0.8 copy-done
  3.0 37.9 %gram.1 = (f32[32,8,256]{2,1,0:T(8,128)S(1)}, bf16[256,256]{1,0:T(8,128)(2,1)S(1)}) custom-call(s32[8,100]{1,0:T(8,128)S(1)} %copy-done.2, f32[4,64]{1,0:T(4,128)S(1)} %copy-done.3, f32[25,64]{1,0:T(8,128)S(1)} %copy-done.1, bf16[64,32]{1,0:T(8,128)(2,1)S(1)} %copy.20.w_ref, f32[1,32]{1,0:T(1,128)S(1)} %bitcast.94, f32[1,32]{1,0:T(1,128)S(1)} %bitcast.95, ...), custom_call_target="tpu_custom_call" | custom-call | tf_op jit(solution)/shard_map/gram/pallas_call | solution.py:221
  41.9 11.7 %cholesky.49 = f32[128,128]{1,0:T(8,128)S(1)} custom-call(f32[128,128]{1,0:T(8,128)S(1)} %cholesky.115), custom_call_target="Cholesky" | custom-call | tf_op jit(solution)/shard_map/jit(cholesky)/cholesky | solution.py:248
  53.7 9.8 %custom-call.18 = f32[1,128,128]{1,2,0:T(8,128)S(1)} custom-call(f32[1,128,128]{2,1,0:T(8,128)S(1)} %get-tuple-element.44), custom_call_target="InvertDiagBlocksLowerTriangular" | custom-call | tf_op jit(solution)/shard_map/jit(cholesky)/cholesky | solution.py:248
  63.5 0.2 fusion.8
  63.7 0.3 convolution_subtract_fusion
  64.0 11.9 %cholesky.103 = f32[128,128]{1,0:T(8,128)S(1)} custom-call(f32[128,128]{1,0:T(8,128)S(1)} %convolution_subtract_fusion), custom_call_target="Cholesky" | custom-call | tf_op jit(solution)/shard_map/jit(cholesky)/cholesky | solution.py:248
  75.9 0.6 compare_reduce_fusion
  78.3 4.2 %while.1 = (s32[]{:T(128)}, f32[256,256]{0,1:T(8,128)S(1)}, s32[2,2]{1,0:T(2,128)S(1)}, f32[2,128,128]{2,1,0:T(8,128)S(1)}, s32[]{:T(128)}) while((s32[]{:T(128)}, f32[256,256]{0,1:T(8,128)S(1)}, s32[2,2]{1,0:T(2,128)S(1)}, f32[2,128,128]{2,1,0:T(8,128)S(1)}, s32[]{:T(128)}) %tuple.29), condition=%wide.while_cond, body=%wide.while_body.sunk | while | flops 2 | bytes 393321 | solution.py:250
  78.3 0.6 fusion.31
  78.9 1.4 %dynamic-slice.8 = f32[128,128]{0,1:T(8,128)S(1)} dynamic-slice(f32[256,256]{0,1:T(8,128)S(1)} %get-tuple-element.87, s32[]{:T(128)} %bitcast.87, s32[]{:T(128)} %bitcast.88), dynamic_slice_sizes={128,128} | dynamic-slice | bytes 131076 | tf_op jit(solution)/shard_map/jit(_cho_solve)/triangular_solve
  80.4 0.6 fusion.31
  81.0 1.4 %dynamic-slice.8 = f32[128,128]{0,1:T(8,128)S(1)} dynamic-slice(f32[256,256]{0,1:T(8,128)S(1)} %get-tuple-element.87, s32[]{:T(128)} %bitcast.87, s32[]{:T(128)} %bitcast.88), dynamic_slice_sizes={128,128} | dynamic-slice | bytes 131076 | tf_op jit(solution)/shard_map/jit(_cho_solve)/triangular_solve
  82.5 19.7 %custom-call.19 = f32[2,128,128]{1,2,0:T(8,128)S(1)} custom-call(f32[2,128,128]{2,1,0:T(8,128)S(1)} %get-tuple-element.18), custom_call_target="InvertDiagBlocksLowerTriangular" | custom-call | tf_op jit(solution)/shard_map/jit(_cho_solve)/triangular_solve | solution.py:250
  102.2 0.6 reduce_sum.9
  104.0 0.2 convolution_bitcast_fusion.2
  104.2 0.2 fusion.1
  104.4 0.2 convolution_bitcast_fusion
  104.8 11.6 %gather.7 = (f32[32,128]{1,0:T(8,128)S(1)}, f32[64,32]{1,0:T(8,128)S(1)}) custom-call(f32[2,128]{1,0:T(2,128)S(1)} %bitcast.93), custom_call_target="tpu_custom_call" | custom-call | tf_op jit(solution)/shard_map/gather/pallas_call | solution.py:253
  116.4 0.7 copy.27
  117.1 0.6 fusion.20
  117.7 0.6 copy.49
  (40 shorter events, 1.7 us)
Async XLA Ops:
  0.6 0.9 copy-start.1
  0.6 0.9 copy-start.2
  1.4 0.7 copy-start.3
  1.5 0.7 copy-start.4
  1.5 0.7 copy-start.5
  2.1 0.8 copy-start
  82.5 19.7 %copy-start.6 = (f32[256]{0:T(256)S(1)}, f32[256]{0:T(256)}, u32[]{:S(2)}) copy-start(f32[256]{0:T(256)} %param.16) | copy-start | bytes 3076

commit v2 on v1

--- a/solution.py
+++ b/solution.py
@@ -21,6 +21,7 @@
 NSAMP = 32
 NPAR = 8
 NX, NZH, NY = 4, 2, 4
+PANEL = 16
 ROWS = PATCHES * OWN
 
 
@@ -58,8 +59,10 @@
     )
     hidden = (jnp.dot(picked, spread, precision=HI, preferred_element_type=F32) + offsets).astype(BF16)
     w_pad[...] = jnp.zeros_like(w_pad)
-    w_pad[0:D, :] = w_ref[...].astype(F32)
-    act = jnp.dot(hidden, w_pad[...].astype(BF16), preferred_element_type=F32) + bias_ref[...]
+    w_pad[:, 0:D] = w_ref[...].astype(F32)
+    act = lax.dot_general(
+        hidden, w_pad[...].astype(BF16), (((1,), (1,)), ((), ())), preferred_element_type=F32
+    ) + bias_ref[...]
     slope_pad[...] = jnp.zeros_like(slope_pad)
     slope_pad[0:ROWS, 0:FOWN] = readout_ref[...] * jnp.tanh(act)
     slope_t = jnp.transpose(slope_pad[...])[0:FOWN, :]
@@ -72,10 +75,94 @@
     return jnp.dot(left, right, precision=HI, preferred_element_type=F32)
 
 
-def gram_kernel(
-    spins_ref, embed_ref, position_ref, w_ref, bias_ref, readout_ref, other_ref,
-    gram_ref, cent_ref,
-    spin_pad, table, w_pad, slope_pad, sbuf, rbuf, cbuf, pair_out, pair_in, half, xy_in, z_in, send_sem, recv_sem,
+def solve(gram_ref, shift, target, upper_ref, scaled_ref):
+    lane = lax.broadcasted_iota(jnp.int32, (8, 128), 1)
+    sub = lax.broadcasted_iota(jnp.int32, (8, 128), 0)
+    tiles = PANEL // 8
+    panels = SAMPLES // PANEL
+    reach = {}
+    for m in range(panels):
+        base = PANEL * m
+        diag, off = base // 128, base % 128
+        for n in (0, 1) if m == 0 else ((m + 1,) if m + 1 < panels else ()):
+            first = PANEL * n
+            owed = None
+            if m:
+                row = lax.broadcasted_iota(jnp.int32, (base, 128), 0)
+                col = lax.broadcasted_iota(jnp.int32, (base, 128), 1)
+                right = []
+                for half in range(2):
+                    part = scaled_ref[0:base, 128 * half : 128 * half + 128]
+                    if half < diag:
+                        part = jnp.where(col + 128 * half <= row, part, 0.0)
+                    elif half == diag:
+                        part = jnp.where((col >= off) | (col + 128 * half <= row), part, 0.0)
+                    right.append(part)
+                owed = lax.dot_general(
+                    upper_ref[0:base, first : first + PANEL], jnp.concatenate(right, axis=1),
+                    (((0,), (0,)), ((), ())), preferred_element_type=F32, precision=HI,
+                )
+            rows = []
+            for tile in range(tiles):
+                pair = []
+                for half in range(2):
+                    part = gram_ref[first // 8 + tile, :, 128 * half : 128 * half + 128]
+                    at = first + 8 * tile - 128 * half
+                    if 0 <= at < 128:
+                        part = jnp.where(lane == sub + at, part + shift, part)
+                    if half < diag:
+                        part = jnp.zeros_like(part)
+                    elif half == diag and off:
+                        part = jnp.where(lane >= off, part, 0.0)
+                    if owed is not None:
+                        part = part - owed[8 * tile : 8 * tile + 8, 128 * half : 128 * half + 128]
+                    pair.append(part)
+                rows.append(pair)
+            reach[n] = rows
+        near = [n for n in (m, m + 1) if n < panels]
+        inside = (lane >= off) & (lane < off + PANEL)
+        column = {}
+        for j in range(PANEL):
+            for n in near:
+                for tile in range(tiles):
+                    column[j, n, tile] = jnp.broadcast_to(reach[n][tile][diag][:, off + j : off + j + 1], (8, 128))
+        for n in near:
+            for tile in range(tiles):
+                reach[n][tile][diag] = jnp.where(inside, 0.0, reach[n][tile][diag])
+        for j in range(PANEL):
+            mine, at = j // 8, j % 8
+            inverse = 1.0 / column[j, m, mine][at : at + 1, :]
+            live = [
+                (n, tile) for n in near for tile in range(tiles)
+                if n > m or tile > mine or (tile == mine and at < 7)
+            ]
+            for k in range(j + 1, PANEL):
+                factor = column[k, m, mine][at : at + 1, :] * inverse
+                for n, tile in live:
+                    column[k, n, tile] = column[k, n, tile] - column[j, n, tile] * factor
+            for half in range(2):
+                pivot_row = reach[m][mine][half][at : at + 1, :]
+                if half == diag:
+                    pivot_row = jnp.where(lane[0:1] == off + j, 1.0, pivot_row)
+                scaled = pivot_row * inverse
+                upper_ref[base + j : base + j + 1, 128 * half : 128 * half + 128] = pivot_row
+                scaled_ref[base + j : base + j + 1, 128 * half : 128 * half + 128] = scaled
+                for n, tile in live:
+                    reach[n][tile][half] = reach[n][tile][half] - column[j, n, tile] * scaled
+        del reach[m]
+    row = lax.broadcasted_iota(jnp.int32, (SAMPLES, SAMPLES), 0)
+    col = lax.broadcasted_iota(jnp.int32, (SAMPLES, SAMPLES), 1)
+    low = col <= row
+    half_solved = jnp.sum(jnp.where(low, upper_ref[...], 0.0) * target, axis=1, keepdims=True)
+    return jnp.sum(jnp.where(low, scaled_ref[...], 0.0) * half_solved, axis=0, keepdims=True)
+
+
+def kernel(
+    spins_hbm, embed_hbm, position_hbm, w_hbm, bias_hbm, readout_hbm, other_hbm, energies_hbm, shift_hbm,
+    coeffs_ref, update_ref, rest_ref,
+    spins_ref, embed_ref, position_ref, w_ref, bias_ref, readout_ref, other_ref, energies_ref, shift_ref,
+    spin_pad, table, w_pad, slope_pad, sbuf, rbuf, cbuf, pair_out, pair_in, half, xy_in, z_in, gram_ref,
+    upper, scaled, result, results, send_sem, recv_sem, load_sem,
 ):
     samp, par, x, zh, y, zl, core = place()
     q = x * 4 + y
@@ -94,6 +181,18 @@
         nz = lax.rem(z + k, 8)
         return nz, (x * 8 + (nz // 4) * 4 + y, (nz % 4) * 2 + core)
 
+    loads = [
+        pltpu.make_async_copy(a, b, load_sem.at[n])
+        for n, (a, b) in enumerate(
+            (
+                (spins_hbm, spins_ref), (embed_hbm, embed_ref), (position_hbm, position_ref), (w_hbm, w_ref),
+                (bias_hbm, bias_ref), (readout_hbm, readout_ref), (other_hbm, other_ref),
+                (energies_hbm, energies_ref), (shift_hbm, shift_ref),
+            )
+        )
+    ]
+    for load in loads:
+        load.start()
     barrier = pltpu.get_barrier_semaphore()
     greeted = 0
     for k in range(1, NSAMP):
@@ -105,6 +204,8 @@
     pl.semaphore_signal(barrier, inc=1, device_id=(samp, mate), device_id_type=MESH)
     greeted += 1
 
+    for load in loads:
+        load.wait()
     grads = local_derivatives(
         spins_ref, embed_ref, position_ref, w_ref, bias_ref, readout_ref, spin_pad, table, w_pad, slope_pad
     )
@@ -135,7 +236,6 @@
     for n, joined in enumerate((others, layer)):
         mean = jnp.sum(joined, axis=0, keepdims=True) / SAMPLES
         cbuf[:, 128 * n : 128 * (n + 1)] = ((joined - mean) * 0.0625).astype(BF16)
-    cent_ref[...] = cbuf[...]
 
     def rows_of(c):
         return lax.dot_general(
@@ -191,42 +291,57 @@
     swap.start()
     swap.wait_recv()
 
-    for ref, n, size in ((sbuf, 0, 31), (pair_out, 1, None), (half, 2, 15), (z_in, 3, 7), (gram_ref, 4, 15), (gram_ref, 5, 16)):
+    energies = energies_ref[...]
+    target = energies - jnp.sum(energies, axis=1, keepdims=True) / SAMPLES
+    x = solve(gram_ref, shift_ref[...], target, upper, scaled)
+    coeffs_ref[...] = pltpu.roll(
+        jnp.broadcast_to(x, (8, SAMPLES)), lax.rem(SAMPLES - OWN * samp, SAMPLES), 1
+    )[0:1, 0:OWN]
+
+    first = x.astype(BF16).astype(F32)
+    second = (x - first).astype(BF16).astype(F32)
+    terms = jnp.concatenate([first, second, x - first - second, jnp.zeros((13, SAMPLES), F32)], axis=0).astype(BF16)
+    full = jnp.dot(terms, cbuf[...], preferred_element_type=F32)
+    full = full[0:1] + (full[1:2] + full[2:3])
+    result[0:1, :] = full[:, 0:128]
+    result[1:2, :] = full[:, 128:256]
+    for k in range(1, NSAMP):
+        pltpu.make_async_remote_copy(
+            src_ref=result, dst_ref=results.at[samp], send_sem=send_sem.at[6], recv_sem=recv_sem.at[6],
+            device_id=samp_peer(k), device_id_type=MESH,
+        ).start()
+    results[samp] = result[...]
+    most = results.at[pl.ds(0, NSAMP - 1)]
+    pltpu.make_async_copy(most, most, recv_sem.at[6]).wait()
+    got = results[...]
+    rest_ref[...] = got[:, 0, :]
+    update_ref[...] = got[:, 1, 0:D]
+
+    for ref, n, size in ((results, 6, 31), (sbuf, 0, 31), (pair_out, 1, None), (half, 2, 15), (z_in, 3, 7), (gram_ref, 4, 15), (gram_ref, 5, 16)):
         part = ref if size is None else ref.at[pl.ds(0, size)]
         pltpu.make_async_copy(part, part, send_sem.at[n]).wait()
 
 
-def gather_kernel(row_ref, rest_ref, layer_ref, recv, send_sem, recv_sem):
-    samp, par = lax.axis_index("samp"), lax.axis_index("par")
-    barrier = pltpu.get_barrier_semaphore()
-    for k in range(1, NSAMP):
-        pl.semaphore_signal(barrier, inc=1, device_id=(lax.rem(samp + k, NSAMP), par), device_id_type=MESH)
-    recv[samp] = row_ref[...]
-    pl.semaphore_wait(barrier, NSAMP - 1)
-    for k in range(1, NSAMP):
-        pltpu.make_async_remote_copy(
-            src_ref=row_ref, dst_ref=recv.at[samp], send_sem=send_sem, recv_sem=recv_sem,
-            device_id=(lax.rem(samp + k, NSAMP), par), device_id_type=MESH,
-        ).start()
-    most = recv.at[pl.ds(0, NSAMP - 1)]
-    pltpu.make_async_copy(most, most, recv_sem).wait()
-    got = recv[...]
-    rest_ref[...] = got[:, 0, :]
-    layer_ref[...] = jnp.transpose(got[:, 1, :])[0:D, :]
-    pltpu.make_async_copy(most, most, send_sem).wait()
-
-
 def per_device(spins, embed, position, w_first, bias_first, readout, other_grads, energies, shift):
     vmem = pl.BlockSpec(memory_space=pltpu.VMEM)
-    gram, cent = pl.pallas_call(
-        gram_kernel,
-        out_shape=(jax.ShapeDtypeStruct((32, 8, 256), F32), jax.ShapeDtypeStruct((256, 256), BF16)),
-        in_specs=[vmem] * 7,
-        out_specs=(vmem, vmem),
-        scratch_shapes=[
+    operands = (
+        spins, embed, position, w_first.T, bias_first.reshape(1, -1), readout.reshape(1, -1), other_grads,
+        energies.reshape(1, -1), shift.reshape(1, 1),
+    )
+    coeffs, update, rest = pl.pallas_call(
+        kernel,
+        out_shape=(
+            jax.ShapeDtypeStruct((1, OWN), F32),
+            jax.ShapeDtypeStruct((FOWN, D), F32),
+            jax.ShapeDtypeStruct((NSAMP, 128), F32),
+        ),
+        in_specs=[pl.BlockSpec(memory_space=pltpu.HBM)] * 9,
+        out_specs=(vmem,) * 3,
+        scratch_shapes=[pltpu.VMEM(a.shape, a.dtype) for a in operands]
+        + [
             pltpu.VMEM((8, 128), F32),
             pltpu.VMEM((40, 128), F32),
-            pltpu.VMEM((128, FOWN), F32),
+            pltpu.VMEM((FOWN, 128), F32),
             pltpu.VMEM((256, 128), F32),
             pltpu.VMEM((NSAMP, 16, 128), BF16),
             pltpu.VMEM((NSAMP, 16, 128), BF16),
@@ -236,36 +351,21 @@
             pltpu.VMEM((16, 8, 256), F32),
             pltpu.VMEM((16, 8, 256), F32),
             pltpu.VMEM((8, 8, 256), F32),
-            pltpu.SemaphoreType.DMA((6,)),
-            pltpu.SemaphoreType.DMA((6,)),
+            pltpu.VMEM((32, 8, 256), F32),
+            pltpu.VMEM((256, 256), F32),
+            pltpu.VMEM((256, 256), F32),
+            pltpu.VMEM((2, 128), F32),
+            pltpu.VMEM((NSAMP, 2, 128), F32),
+            pltpu.SemaphoreType.DMA((7,)),
+            pltpu.SemaphoreType.DMA((7,)),
+            pltpu.SemaphoreType.DMA((9,)),
         ],
         compiler_params=pltpu.CompilerParams(
             collective_id=0, has_side_effects=True, vmem_limit_bytes=32 * 2**20
         ),
-        name="gram",
-    )(spins, embed, position, w_first, bias_first.reshape(1, -1), readout.reshape(1, -1), other_grads)
-    matrix = gram.reshape(SAMPLES, SAMPLES) + shift[0] * jnp.eye(SAMPLES, dtype=F32)
-    lower = jnp.linalg.cholesky(matrix)
-    target = energies - jnp.sum(energies) / SAMPLES
-    solved = jax.scipy.linalg.cho_solve((lower, True), target)
-    coeffs = lax.dynamic_slice_in_dim(solved, lax.axis_index("samp") * OWN, OWN, 0)
-    row = jnp.dot(solved, cent.astype(F32), precision=HI).reshape(2, 128)
-    rest, layer = pl.pallas_call(
-        gather_kernel,
-        out_shape=(jax.ShapeDtypeStruct((NSAMP, 128), F32), jax.ShapeDtypeStruct((D, FOWN), F32)),
-        in_specs=[vmem],
-        out_specs=(vmem, vmem),
-        scratch_shapes=[
-            pltpu.VMEM((NSAMP, 2, 128), F32),
-            pltpu.SemaphoreType.DMA,
-            pltpu.SemaphoreType.DMA,
-        ],
-        compiler_params=pltpu.CompilerParams(
-            collective_id=1, has_side_effects=True, vmem_limit_bytes=32 * 2**20
-        ),
-        name="gather",
-    )(row)
-    return (coeffs, layer, rest.reshape(-1))
+        name="update",
+    )(*operands)
+    return (coeffs.reshape(-1), update.T, rest.reshape(-1))
 
 
 def solution(mesh):

time: 119 us -> 58.3 us (0.49)
  other arithmetic: 55.1 us -> 0 us
  local copies, waits for them, and re-layouts: 8.39 us -> 5.96 us
  between operations: 3.48 us -> 1.33 us
  matrix products: 1.79 us -> 0 us
  Pallas kernels: 49.5 us -> 50.7 us
    another operation x9 -> x0, other arithmetic: 53.8 us -> none  [the longest x6 34.1 us: per_device(): lower = jnp.linalg.cholesky(matrix)]
    another operation x18 -> x0, local copies, waits for them, and re-layouts: 4.54 us -> none
    unnamed x17 -> x19, local copies, waits for them, and re-layouts: 3.59 us -> 5.96 us
    another operation x8 -> x0, matrix products: 1.61 us -> none  [the longest x6 1.14 us: per_device(): solved = jax.scipy.linalg.cho_solve((lower, True), target)]
    pallas_call x2 -> x1, Pallas kernels: 49.5 us -> 50.7 us  [per_device(): pl.pallas_call(kernel, out_shape=(jax.ShapeDtypeStruct((1, OWN), F32), ja...]
where the time goes in v2:
time: 58.3 us; the launch traced here: 58 us
  Pallas kernels  50.7 us (87%)
  local copies, waits for them, and re-layouts  5.96 us (10%)
  between operations  1.33 us (2%)
    pallas_call x1, Pallas kernels, per_device(): pl.pallas_call(kernel, out_shape=(jax.ShapeDtypeStruct((1, OWN), F32), ja...  50.7 us
    unnamed x19, local copies, waits for them, and re-layouts  5.96 us

profile of v2, /device:TPU:1, one launch (start us, length us, event | category | flops | bytes accessed | tf_op | source)
XLA Modules:
  0.0 58.0 jit_solution(10373583203278983662)
XLA Ops:
  0.6 0.0 copy-start.2
  1.3 0.0 copy-start.4
  1.3 0.0 copy-start.5
  1.3 0.0 copy-done.2
  1.3 0.7 %copy-done.4 = f32[4,64]{1,0:T(4,128)S(1)} copy-done((f32[4,64]{1,0:T(4,128)S(1)}, f32[4,64]{1,0:T(4,128)}, u32[]{:S(2)}) %copy-start.4) | copy-done | bytes 1048
  2.0 0.0 copy-done.5
  2.0 0.0 copy-start
  2.0 0.8 %copy-done = bf16[8,4096]{1,0:T(8,128)(2,1)S(1)} copy-done((bf16[8,4096]{1,0:T(8,128)(2,1)S(1)}, bf16[8,4096]{1,0:T(8,128)(2,1)}, u32[]{:S(2)}) %copy-start) | copy-done | bytes 65560
  2.8 0.0 copy-start.1
  2.8 0.7 %copy-done.1 = f32[25,64]{1,0:T(8,128)S(1)} copy-done((f32[25,64]{1,0:T(8,128)S(1)}, f32[25,64]{1,0:T(8,128)}, u32[]{:S(2)}) %copy-start.1) | copy-done | bytes 6424
  3.6 0.0 copy-start.3
  3.6 0.7 %copy-done.3 = s32[8,100]{1,0:T(8,128)S(1)} copy-done((s32[8,100]{1,0:T(8,128)S(1)}, s32[8,100]{1,0:T(8,128)}, u32[]{:S(2)}) %copy-start.3) | copy-done | bytes 3224
  4.2 0.0 copy-start.6
  4.2 0.7 %copy-done.6 = f32[32]{0:T(128)S(1)} copy-done((f32[32]{0:T(128)S(1)}, f32[32]{0:T(128)}, u32[]{:S(2)}) %copy-start.6) | copy-done | bytes 152
  4.9 0.0 copy-start.7
  4.9 0.7 %copy-done.7 = f32[32]{0:T(128)S(1)} copy-done((f32[32]{0:T(128)S(1)}, f32[32]{0:T(128)}, u32[]{:S(2)}) %copy-start.7) | copy-done | bytes 152
  5.6 50.7 %update.1 = (f32[1,8]{1,0:T(1,128)S(1)}, f32[32,64]{1,0:T(8,128)S(1)}, f32[32,128]{1,0:T(8,128)S(1)}) custom-call(s32[8,100]{1,0:T(8,128)S(1)} %copy-done.3, f32[4,64]{1,0:T(4,128)S(1)} %copy-done.4, f32[25,64]{1,0:T(8,128)S(1)} %copy-done.1, bf16[32,64]{1,0:T(8,128)(2,1)S(1)} %bitcast.11, f32[1,32]{1,0:T(1,128)S(1)} %bitcast.13, f32[1,32]{1,0:T(1,128)S(1)} %bitcast.14, ...), custom_call_target="tpu_custom_call" | custom-call | tf_op jit(solution)/shard_map/update/pallas_call | solution.py:331
  56.2 0.5 copy.16
  56.7 0.6 %copy.17 = f32[64,32]{0,1:T(8,128)} copy(f32[64,32]{0,1:T(8,128)S(1)} %bitcast.10) | data formatting | bytes 16384
  57.3 0.6 %copy.18 = f32[4096]{0:T(1024)} copy(f32[4096]{0:T(1024)S(1)} %bitcast.9) | data formatting | bytes 32768
Async XLA Ops:
  0.6 0.7 %copy-start.2 = (bf16[64,32]{0,1:T(8,128)(2,1)S(1)}, bf16[64,32]{0,1:T(8,128)(2,1)}, u32[]{:S(2)}) copy-start(bf16[64,32]{0,1:T(8,128)(2,1)} %param.12) | copy-start | bytes 12292
  1.3 0.7 %copy-start.4 = (f32[4,64]{1,0:T(4,128)S(1)}, f32[4,64]{1,0:T(4,128)}, u32[]{:S(2)}) copy-start(f32[4,64]{1,0:T(4,128)} %embed_hbm.1) | copy-start | bytes 3076
  1.3 0.7 %copy-start.5 = (f32[256]{0:T(256)S(1)}, f32[256]{0:T(256)}, u32[]{:S(2)}) copy-start(f32[256]{0:T(256)} %param.16) | copy-start | bytes 3076
  2.0 0.8 %copy-start = (bf16[8,4096]{1,0:T(8,128)(2,1)S(1)}, bf16[8,4096]{1,0:T(8,128)(2,1)}, u32[]{:S(2)}) copy-start(bf16[8,4096]{1,0:T(8,128)(2,1)} %other_hbm.1) | copy-start | bytes 196612
  2.8 0.7 %copy-start.1 = (f32[25,64]{1,0:T(8,128)S(1)}, f32[25,64]{1,0:T(8,128)}, u32[]{:S(2)}) copy-start(f32[25,64]{1,0:T(8,128)} %position_hbm.1) | copy-start | bytes 19204
  3.6 0.7 %copy-start.3 = (s32[8,100]{1,0:T(8,128)S(1)}, s32[8,100]{1,0:T(8,128)}, u32[]{:S(2)}) copy-start(s32[8,100]{1,0:T(8,128)} %spins_hbm.1) | copy-start | bytes 9604
  4.2 0.7 %copy-start.6 = (f32[32]{0:T(128)S(1)}, f32[32]{0:T(128)}, u32[]{:S(2)}) copy-start(f32[32]{0:T(128)} %param.13) | copy-start | bytes 388
  4.9 0.7 %copy-start.7 = (f32[32]{0:T(128)S(1)}, f32[32]{0:T(128)}, u32[]{:S(2)}) copy-start(f32[32]{0:T(128)} %param.14) | copy-start | bytes 388

commit v3 on v2

--- a/solution.py
+++ b/solution.py
@@ -1,4 +1,4 @@
-import functools
+import itertools
 
 import jax
 import jax.numpy as jnp
@@ -73,6 +73,17 @@
     left = left.reshape(FOWN * OWN, 256)
     right = jnp.concatenate([hidden.astype(F32), jnp.zeros((256 - ROWS, 128), F32)], axis=0)
     return jnp.dot(left, right, precision=HI, preferred_element_type=F32)
+
+
+def gram_tile(gram_ref, row, half):
+    return gram_ref[(row // 8) % 2, (row % 8) * 2 + half, row // 16]
+
+
+def offsets(dims):
+    def far(step):
+        return sum(4 * d if name == "zh" else min(d, 4 - d) for name, d in zip(dims, step))
+    sizes = [2 if name == "zh" else 4 for name in dims]
+    return sorted(itertools.product(*map(range, sizes)), key=far, reverse=True)[:-1]
 
 
 def solve(gram_ref, shift, target, upper_ref, scaled_ref):
@@ -106,7 +117,7 @@
             for tile in range(tiles):
                 pair = []
                 for half in range(2):
-                    part = gram_ref[first // 8 + tile, :, 128 * half : 128 * half + 128]
+                    part = gram_tile(gram_ref, first // 8 + tile, half)
                     at = first + 8 * tile - 128 * half
                     if 0 <= at < 128:
                         part = jnp.where(lane == sub + at, part + shift, part)
@@ -167,20 +178,28 @@
     samp, par, x, zh, y, zl, core = place()
     q = x * 4 + y
     z = zh * 4 + zl
-    mate = zl * 2 + (1 - core)
-
-    def samp_peer(k):
-        return (lax.rem(samp + k, NSAMP), par)
-
-    def xy_peer(k):
-        nx = lax.rem(x + k // 4, 4)
-        ny = lax.rem(y + k % 4, 4)
-        return nx * 4 + ny, (nx * 8 + zh * 4 + ny, par)
+    mate = (samp, zl * 2 + (1 - core))
+
+    def samp_peer(step):
+        dx, dz, dy = step
+        nq = lax.rem(x + dx, 4) * 4 + lax.rem(y + dy, 4)
+        return nq, ((nq // 4) * 8 + lax.rem(zh + dz, 2) * 4 + nq % 4, par)
+
+    def xy_peer(step):
+        return samp_peer((step[0], 0, step[1]))
 
     def z_peer(k):
         nz = lax.rem(z + k, 8)
-        return nz, (x * 8 + (nz // 4) * 4 + y, (nz % 4) * 2 + core)
-
+        return (x * 8 + (nz // 4) * 4 + y, (nz % 4) * 2 + core)
+
+    plane = offsets(("x", "y"))
+    group = offsets(("x", "zh", "y"))
+    column = (4, 3, 5, 2, 6, 1, 7)
+
+    barrier = pltpu.get_barrier_semaphore()
+    greet = [samp_peer(step)[1] for step in group] + [z_peer(k) for k in column if k != 4] + [mate]
+    for to in greet:
+        pl.semaphore_signal(barrier, inc=1, device_id=to, device_id_type=MESH)
     loads = [
         pltpu.make_async_copy(a, b, load_sem.at[n])
         for n, (a, b) in enumerate(
@@ -193,68 +212,67 @@
     ]
     for load in loads:
         load.start()
-    barrier = pltpu.get_barrier_semaphore()
-    greeted = 0
-    for k in range(1, NSAMP):
-        pl.semaphore_signal(barrier, inc=1, device_id=samp_peer(k), device_id_type=MESH)
-        greeted += 1
-    for k in (1, 2, 3, 5, 6, 7):
-        pl.semaphore_signal(barrier, inc=1, device_id=z_peer(k)[1], device_id_type=MESH)
-        greeted += 1
-    pl.semaphore_signal(barrier, inc=1, device_id=(samp, mate), device_id_type=MESH)
-    greeted += 1
-
     for load in loads:
         load.wait()
+
     grads = local_derivatives(
         spins_ref, embed_ref, position_ref, w_ref, bias_ref, readout_ref, spin_pad, table, w_pad, slope_pad
-    )
-    lane = lax.broadcasted_iota(jnp.int32, (256, 128), 1)
-    high = grads.astype(BF16).astype(F32)
-    terms = jnp.where(lane < D, high, grads - high)
-    for j in range(NSAMP):
-        sbuf[j] = jnp.concatenate(
-            [other_ref[:, 128 * j : 128 * (j + 1)].astype(F32), terms[8 * j : 8 * (j + 1), :]], axis=0
+    ).reshape(16, 2, OWN, 128)
+    lane = lax.broadcasted_iota(jnp.int32, (16, OWN, 128), 2)
+    own = jnp.where(lane < D, grads[:, 0], grads[:, 1])
+    high = own.astype(BF16).astype(F32)
+    low = own - high
+    for n in range(16):
+        sbuf[n] = jnp.concatenate(
+            [
+                other_ref[:, 256 * n : 256 * n + 128].astype(F32),
+                other_ref[:, 256 * n + 128 : 256 * n + 256].astype(F32),
+                high[n],
+                low[n],
+            ],
+            axis=0,
         ).astype(BF16)
 
-    pl.semaphore_wait(barrier, greeted)
-
-    for k in range(1, NSAMP):
-        to = samp_peer(k)
-        pltpu.make_async_remote_copy(
-            src_ref=sbuf.at[to[0]], dst_ref=rbuf.at[samp], send_sem=send_sem.at[0], recv_sem=recv_sem.at[0],
+    pl.semaphore_wait(barrier, len(greet))
+
+    for step in group:
+        nq, to = samp_peer(step)
+        pltpu.make_async_remote_copy(
+            src_ref=sbuf.at[nq], dst_ref=rbuf.at[samp], send_sem=send_sem.at[0], recv_sem=recv_sem.at[0],
             device_id=to, device_id_type=MESH,
         ).start()
-    rbuf[samp] = sbuf[samp]
+    rbuf[samp] = sbuf[q]
     most = rbuf.at[pl.ds(0, NSAMP - 1)]
     pltpu.make_async_copy(most, most, recv_sem.at[0]).wait()
 
     got = rbuf[...].astype(F32)
-    others = got[:, 0:8, :].reshape(SAMPLES, 128)
-    pair = got[:, 8:16, :].reshape(SAMPLES, 128)
-    layer = jnp.where(lane < D, pair + pltpu.roll(pair, D, 1), 0.0)
-    for n, joined in enumerate((others, layer)):
+    parts = [got[:, 8 * n : 8 * n + 8, :].reshape(SAMPLES, 128) for n in range(4)]
+    for n, joined in enumerate((parts[0], parts[1], parts[2] + parts[3])):
         mean = jnp.sum(joined, axis=0, keepdims=True) / SAMPLES
         cbuf[:, 128 * n : 128 * (n + 1)] = ((joined - mean) * 0.0625).astype(BF16)
 
     def rows_of(c):
+        first = pl.multiple_of(zh * 128 + c * 64, 64)
         return lax.dot_general(
-            cbuf[pl.ds(pl.multiple_of(c * 128, 128), 128), :], cbuf[...], (((1,), (1,)), ((), ())),
-            preferred_element_type=F32,
+            cbuf[pl.ds(first, 64), :], cbuf[...], (((1,), (1,)), ((), ())), preferred_element_type=F32
         )
 
-    pair_out[...] = rows_of(1 - core)
+    theirs = rows_of(1 - core)
+    for n in range(16):
+        pair_out[n] = theirs[8 * (n // 2) : 8 * (n // 2) + 8, 128 * (n % 2) : 128 * (n % 2) + 128]
     swap = pltpu.make_async_remote_copy(
         src_ref=pair_out, dst_ref=pair_in, send_sem=send_sem.at[1], recv_sem=recv_sem.at[1],
-        device_id=(samp, mate), device_id_type=MESH,
+        device_id=mate, device_id_type=MESH,
     )
     swap.start()
-    own = rows_of(core)
+    ours = rows_of(core)
+    for n in range(16):
+        half[n] = ours[8 * (n // 2) : 8 * (n // 2) + 8, 128 * (n % 2) : 128 * (n % 2) + 128]
     swap.wait_recv()
-    half[...] = (own + pair_in[...]).reshape(16, 8, 256)
-
-    for k in range(1, 16):
-        nq, to = xy_peer(k)
+    half[...] += pair_in[...]
+
+    for step in plane:
+        nq, to = xy_peer(step)
         pltpu.make_async_remote_copy(
             src_ref=half.at[nq], dst_ref=xy_in.at[q], send_sem=send_sem.at[2], recv_sem=recv_sem.at[2],
             device_id=to, device_id_type=MESH,
@@ -264,61 +282,60 @@
     pltpu.make_async_copy(most, most, recv_sem.at[2]).wait()
     z_in[z] = jnp.sum(xy_in[...], axis=0)
 
-    for k in range(1, 8):
-        to = z_peer(k)[1]
+    for k in column:
         pltpu.make_async_remote_copy(
             src_ref=z_in.at[z], dst_ref=z_in.at[z], send_sem=send_sem.at[3], recv_sem=recv_sem.at[3],
-            device_id=to, device_id_type=MESH,
+            device_id=z_peer(k), device_id_type=MESH,
         ).start()
     most = z_in.at[pl.ds(0, 7)]
     pltpu.make_async_copy(most, most, recv_sem.at[3]).wait()
-    mine = core * 16 + q
-    gram_ref[mine] = jnp.sum(z_in[...], axis=0)
-
-    for k in range(1, 16):
-        to = xy_peer(k)[1]
-        pltpu.make_async_remote_copy(
-            src_ref=gram_ref.at[mine], dst_ref=gram_ref.at[mine], send_sem=send_sem.at[4], recv_sem=recv_sem.at[4],
-            device_id=to, device_id_type=MESH,
-        ).start()
-    most = gram_ref.at[pl.ds(core * 16, 15)]
+    for n in range(2):
+        gram_ref[core, q, n] = jnp.sum(z_in[4 * n : 4 * n + 4], axis=0)
+
+    for step in plane:
+        pltpu.make_async_remote_copy(
+            src_ref=gram_ref.at[core, q], dst_ref=gram_ref.at[core, q], send_sem=send_sem.at[4],
+            recv_sem=recv_sem.at[4], device_id=xy_peer(step)[1], device_id_type=MESH,
+        ).start()
+    most = gram_ref.at[core, pl.ds(0, 15)]
     pltpu.make_async_copy(most, most, recv_sem.at[4]).wait()
-    own_half = gram_ref.at[pl.ds(core * 16, 16)]
     swap = pltpu.make_async_remote_copy(
-        src_ref=own_half, dst_ref=own_half, send_sem=send_sem.at[5], recv_sem=recv_sem.at[5],
-        device_id=(samp, mate), device_id_type=MESH,
+        src_ref=gram_ref.at[core], dst_ref=gram_ref.at[core], send_sem=send_sem.at[5], recv_sem=recv_sem.at[5],
+        device_id=mate, device_id_type=MESH,
     )
     swap.start()
     swap.wait_recv()
 
     energies = energies_ref[...]
     target = energies - jnp.sum(energies, axis=1, keepdims=True) / SAMPLES
-    x = solve(gram_ref, shift_ref[...], target, upper, scaled)
+    x_row = solve(gram_ref, shift_ref[...], target, upper, scaled)
     coeffs_ref[...] = pltpu.roll(
-        jnp.broadcast_to(x, (8, SAMPLES)), lax.rem(SAMPLES - OWN * samp, SAMPLES), 1
+        jnp.broadcast_to(x_row, (8, SAMPLES)), lax.rem(SAMPLES - OWN * samp, SAMPLES), 1
     )[0:1, 0:OWN]
 
-    first = x.astype(BF16).astype(F32)
-    second = (x - first).astype(BF16).astype(F32)
-    terms = jnp.concatenate([first, second, x - first - second, jnp.zeros((13, SAMPLES), F32)], axis=0).astype(BF16)
+    first = x_row.astype(BF16).astype(F32)
+    second = (x_row - first).astype(BF16).astype(F32)
+    terms = jnp.concatenate([first, second, x_row - first - second, jnp.zeros((13, SAMPLES), F32)], axis=0).astype(BF16)
     full = jnp.dot(terms, cbuf[...], preferred_element_type=F32)
     full = full[0:1] + (full[1:2] + full[2:3])
-    result[0:1, :] = full[:, 0:128]
-    result[1:2, :] = full[:, 128:256]
-    for k in range(1, NSAMP):
-        pltpu.make_async_remote_copy(
-            src_ref=result, dst_ref=results.at[samp], send_sem=send_sem.at[6], recv_sem=recv_sem.at[6],
-            device_id=samp_peer(k), device_id_type=MESH,
-        ).start()
-    results[samp] = result[...]
-    most = results.at[pl.ds(0, NSAMP - 1)]
+    for n in range(3):
+        result[n : n + 1, :] = full[:, 128 * n : 128 * n + 128]
+    result[3:4, :] = full[:, 0:128]
+    for step in plane:
+        pltpu.make_async_remote_copy(
+            src_ref=result, dst_ref=results.at[q], send_sem=send_sem.at[6], recv_sem=recv_sem.at[6],
+            device_id=xy_peer(step)[1], device_id_type=MESH,
+        ).start()
+    results[q] = result[...]
+    most = results.at[pl.ds(0, 15)]
     pltpu.make_async_copy(most, most, recv_sem.at[6]).wait()
-    got = results[...]
-    rest_ref[...] = got[:, 0, :]
-    update_ref[...] = got[:, 1, 0:D]
-
-    for ref, n, size in ((results, 6, 31), (sbuf, 0, 31), (pair_out, 1, None), (half, 2, 15), (z_in, 3, 7), (gram_ref, 4, 15), (gram_ref, 5, 16)):
-        part = ref if size is None else ref.at[pl.ds(0, size)]
+    rest_ref[...] = results[:, 0:2, :]
+    update_ref[...] = results[:, 2, :]
+
+    for part, n in (
+        (rbuf.at[pl.ds(0, 31)], 0), (pair_out, 1), (half.at[pl.ds(0, 15)], 2), (z_in.at[pl.ds(0, 7)], 3),
+        (gram_ref.at[0, pl.ds(0, 15)], 4), (gram_ref.at[0], 5), (results.at[pl.ds(0, 15)], 6),
+    ):
         pltpu.make_async_copy(part, part, send_sem.at[n]).wait()
 
 
@@ -328,12 +345,13 @@
         spins, embed, position, w_first.T, bias_first.reshape(1, -1), readout.reshape(1, -1), other_grads,
         energies.reshape(1, -1), shift.reshape(1, 1),
     )
+    operands = tuple(pltpu.with_memory_space_constraint(a, pltpu.HBM) for a in operands[:-1]) + operands[-1:]
     coeffs, update, rest = pl.pallas_call(
         kernel,
         out_shape=(
             jax.ShapeDtypeStruct((1, OWN), F32),
-            jax.ShapeDtypeStruct((FOWN, D), F32),
-            jax.ShapeDtypeStruct((NSAMP, 128), F32),
+            jax.ShapeDtypeStruct((16, 128), F32),
+            jax.ShapeDtypeStruct((16, 2, 128), F32),
         ),
         in_specs=[pl.BlockSpec(memory_space=pltpu.HBM)] * 9,
         out_specs=(vmem,) * 3,
@@ -343,19 +361,19 @@
             pltpu.VMEM((40, 128), F32),
             pltpu.VMEM((FOWN, 128), F32),
             pltpu.VMEM((256, 128), F32),
-            pltpu.VMEM((NSAMP, 16, 128), BF16),
-            pltpu.VMEM((NSAMP, 16, 128), BF16),
-            pltpu.VMEM((256, 256), BF16),
-            pltpu.VMEM((128, 256), F32),
-            pltpu.VMEM((128, 256), F32),
-            pltpu.VMEM((16, 8, 256), F32),
-            pltpu.VMEM((16, 8, 256), F32),
-            pltpu.VMEM((8, 8, 256), F32),
-            pltpu.VMEM((32, 8, 256), F32),
-            pltpu.VMEM((256, 256), F32),
-            pltpu.VMEM((256, 256), F32),
-            pltpu.VMEM((2, 128), F32),
-            pltpu.VMEM((NSAMP, 2, 128), F32),
+            pltpu.VMEM((16, 32, 128), BF16),
+            pltpu.VMEM((NSAMP, 32, 128), BF16),
+            pltpu.VMEM((SAMPLES, 384), BF16),
+            pltpu.VMEM((16, 8, 128), F32),
+            pltpu.VMEM((16, 8, 128), F32),
+            pltpu.VMEM((16, 8, 128), F32),
+            pltpu.VMEM((16, 8, 128), F32),
+            pltpu.VMEM((8, 8, 128), F32),
+            pltpu.VMEM((2, 16, 2, 8, 128), F32),
+            pltpu.VMEM((SAMPLES, SAMPLES), F32),
+            pltpu.VMEM((SAMPLES, SAMPLES), F32),
+            pltpu.VMEM((4, 128), F32),
+            pltpu.VMEM((16, 4, 128), F32),
             pltpu.SemaphoreType.DMA((7,)),
             pltpu.SemaphoreType.DMA((7,)),
             pltpu.SemaphoreType.DMA((9,)),
@@ -365,7 +383,7 @@
         ),
         name="update",
     )(*operands)
-    return (coeffs.reshape(-1), update.T, rest.reshape(-1))
+    return (coeffs.reshape(-1), update.reshape(FOWN, D).T, rest.reshape(-1))
 
 
 def solution(mesh):

time: 58.3 us -> 52.8 us (0.906)
  local copies, waits for them, and re-layouts: 5.96 us -> 1.79 us
  Pallas kernels: 50.7 us -> 49.5 us
    unnamed x19 -> x2, local copies, waits for them, and re-layouts: 5.96 us -> 1.12 us
    pallas_call x1, Pallas kernels: 50.7 us -> 49.5 us  [per_device(): pl.pallas_call(kernel, out_shape=(jax.ShapeDtypeStruct((1, OWN), F32), ja...]
    reshape x0 -> x1, local copies, waits for them, and re-layouts: none -> 0.68 us  [per_device(): return (coeffs.reshape(-1), update.reshape(FOWN, D).T, rest.reshape(-1))]
where the time goes in v3:
time: 52.8 us; the launch traced here: 52.6 us
  Pallas kernels  49.5 us (94%)
  local copies, waits for them, and re-layouts  1.79 us (3%)
  between operations  1.29 us (2%)
    pallas_call x1, Pallas kernels, per_device(): pl.pallas_call(kernel, out_shape=(jax.ShapeDtypeStruct((1, OWN), F32), ja...  49.5 us
    unnamed x2, local copies, waits for them, and re-layouts  1.12 us

profile of v3, /device:TPU:1, one launch (start us, length us, event | category | flops | bytes accessed | tf_op | source)
XLA Modules:
  0.0 52.6 jit_solution(3808884726364072973)
XLA Ops:
  1.3 49.5 %update.1 = (f32[1,8]{1,0:T(1,128)S(1)}, f32[16,128]{1,0:T(8,128)S(1)}, f32[16,2,128]{2,1,0:T(2,128)S(1)}) custom-call(s32[8,100]{1,0:T(8,128)} %spins_hbm.1, f32[4,64]{1,0:T(4,128)} %embed_hbm.1, f32[25,64]{1,0:T(8,128)} %position_hbm.1, bf16[32,64]{1,0:T(8,128)(2,1)} %bitcast.12, f32[1,32]{1,0:T(1,128)} %bitcast.14, f32[1,32]{1,0:T(1,128)} %bitcast.15, ...), custom_call_target="tpu_custom_call" | custom-call | tf_op jit(solution)/shard_map/update/pallas_call | solution.py:349
  50.8 0.7 %reshape.32 = f32[32,64]{1,0:T(8,128)} reshape(f32[16,128]{1,0:T(8,128)S(1)} %get-tuple-element.7) | data formatting | bytes 16384 | tf_op jit(solution)/shard_map/reshape | solution.py:386
  51.5 0.5 copy.15
  52.0 0.6 %copy.16 = f32[4096]{0:T(1024)} copy(f32[4096]{0:T(1024)S(1)} %bitcast.9) | data formatting | bytes 32768

commit v4 on v3

--- a/solution.py
+++ b/solution.py
@@ -75,15 +75,11 @@
     return jnp.dot(left, right, precision=HI, preferred_element_type=F32)
 
 
-def gram_tile(gram_ref, row, half):
-    return gram_ref[(row // 8) % 2, (row % 8) * 2 + half, row // 16]
-
-
 def offsets(dims):
     def far(step):
-        return sum(4 * d if name == "zh" else min(d, 4 - d) for name, d in zip(dims, step))
-    sizes = [2 if name == "zh" else 4 for name in dims]
-    return sorted(itertools.product(*map(range, sizes)), key=far, reverse=True)[:-1]
+        return sum({"zh": 4 * d, "core": 0}.get(name, min(d, 4 - d)) for name, d in zip(dims, step))
+    sizes = [4 if name in "xy" else 2 for name in dims]
+    return sorted(filter(any, itertools.product(*map(range, sizes))), key=far, reverse=True)
 
 
 def solve(gram_ref, shift, target, upper_ref, scaled_ref):
@@ -117,7 +113,7 @@
             for tile in range(tiles):
                 pair = []
                 for half in range(2):
-                    part = gram_tile(gram_ref, first // 8 + tile, half)
+                    part = gram_ref[first // 8 + tile, :, 128 * half : 128 * half + 128]
                     at = first + 8 * tile - 128 * half
                     if 0 <= at < 128:
                         part = jnp.where(lane == sub + at, part + shift, part)
@@ -172,32 +168,37 @@
     spins_hbm, embed_hbm, position_hbm, w_hbm, bias_hbm, readout_hbm, other_hbm, energies_hbm, shift_hbm,
     coeffs_ref, update_ref, rest_ref,
     spins_ref, embed_ref, position_ref, w_ref, bias_ref, readout_ref, other_ref, energies_ref, shift_ref,
-    spin_pad, table, w_pad, slope_pad, sbuf, rbuf, cbuf, pair_out, pair_in, half, xy_in, z_in, gram_ref,
+    spin_pad, table, w_pad, slope_pad, sbuf, rbuf, cbuf, gram_part, plane_in, z_in, gram_ref,
     upper, scaled, result, results, send_sem, recv_sem, load_sem,
 ):
     samp, par, x, zh, y, zl, core = place()
     q = x * 4 + y
     z = zh * 4 + zl
-    mate = (samp, zl * 2 + (1 - core))
+    mine = q * 2 + core
+    owner = zh == zl // 3
 
     def samp_peer(step):
         dx, dz, dy = step
         nq = lax.rem(x + dx, 4) * 4 + lax.rem(y + dy, 4)
         return nq, ((nq // 4) * 8 + lax.rem(zh + dz, 2) * 4 + nq % 4, par)
 
-    def xy_peer(step):
-        return samp_peer((step[0], 0, step[1]))
+    def plane_peer(step):
+        dx, dy, dc = step
+        nq, (to, _) = samp_peer((dx, 0, dy))
+        nc = lax.rem(core + dc, 2)
+        return nq * 2 + nc, (to, zl * 2 + nc)
 
     def z_peer(k):
         nz = lax.rem(z + k, 8)
         return (x * 8 + (nz // 4) * 4 + y, (nz % 4) * 2 + core)
 
-    plane = offsets(("x", "y"))
     group = offsets(("x", "zh", "y"))
+    plane = offsets(("x", "y", "core"))
     column = (4, 3, 5, 2, 6, 1, 7)
 
     barrier = pltpu.get_barrier_semaphore()
-    greet = [samp_peer(step)[1] for step in group] + [z_peer(k) for k in column if k != 4] + [mate]
+    greet = [samp_peer(step)[1] for step in group] + [z_peer(k) for k in column if k != 4]
+    greet += [plane_peer(step)[1] for step in plane if step[2]]
     for to in greet:
         pl.semaphore_signal(barrier, inc=1, device_id=to, device_id_type=MESH)
     loads = [
@@ -251,60 +252,43 @@
         mean = jnp.sum(joined, axis=0, keepdims=True) / SAMPLES
         cbuf[:, 128 * n : 128 * (n + 1)] = ((joined - mean) * 0.0625).astype(BF16)
 
-    def rows_of(c):
-        first = pl.multiple_of(zh * 128 + c * 64, 64)
-        return lax.dot_general(
-            cbuf[pl.ds(first, 64), :], cbuf[...], (((1,), (1,)), ((), ())), preferred_element_type=F32
-        )
-
-    theirs = rows_of(1 - core)
-    for n in range(16):
-        pair_out[n] = theirs[8 * (n // 2) : 8 * (n // 2) + 8, 128 * (n % 2) : 128 * (n % 2) + 128]
-    swap = pltpu.make_async_remote_copy(
-        src_ref=pair_out, dst_ref=pair_in, send_sem=send_sem.at[1], recv_sem=recv_sem.at[1],
-        device_id=mate, device_id_type=MESH,
-    )
-    swap.start()
-    ours = rows_of(core)
-    for n in range(16):
-        half[n] = ours[8 * (n // 2) : 8 * (n // 2) + 8, 128 * (n % 2) : 128 * (n % 2) + 128]
-    swap.wait_recv()
-    half[...] += pair_in[...]
-
-    for step in plane:
-        nq, to = xy_peer(step)
-        pltpu.make_async_remote_copy(
-            src_ref=half.at[nq], dst_ref=xy_in.at[q], send_sem=send_sem.at[2], recv_sem=recv_sem.at[2],
-            device_id=to, device_id_type=MESH,
-        ).start()
-    xy_in[q] = half[q]
-    most = xy_in.at[pl.ds(0, 15)]
-    pltpu.make_async_copy(most, most, recv_sem.at[2]).wait()
-    z_in[z] = jnp.sum(xy_in[...], axis=0)
-
-    for k in column:
-        pltpu.make_async_remote_copy(
-            src_ref=z_in.at[z], dst_ref=z_in.at[z], send_sem=send_sem.at[3], recv_sem=recv_sem.at[3],
-            device_id=z_peer(k), device_id_type=MESH,
-        ).start()
-    most = z_in.at[pl.ds(0, 7)]
-    pltpu.make_async_copy(most, most, recv_sem.at[3]).wait()
-    for n in range(2):
-        gram_ref[core, q, n] = jnp.sum(z_in[4 * n : 4 * n + 4], axis=0)
+    @pl.when(owner)
+    def _():
+        gram_part[...] = lax.dot_general(
+            cbuf[...], cbuf[...], (((1,), (1,)), ((), ())), preferred_element_type=F32
+        ).reshape(32, 8, SAMPLES)
+        for step in plane:
+            to, device = plane_peer(step)
+            pltpu.make_async_remote_copy(
+                src_ref=gram_part.at[to], dst_ref=plane_in.at[mine], send_sem=send_sem.at[1], recv_sem=recv_sem.at[1],
+                device_id=device, device_id_type=MESH,
+            ).start()
+        plane_in[mine] = gram_part[mine]
+        most = plane_in.at[pl.ds(0, 31)]
+        pltpu.make_async_copy(most, most, recv_sem.at[1]).wait()
+        z_in[zl] = jnp.sum(plane_in[...], axis=0)
+
+        for k in column:
+            pltpu.make_async_remote_copy(
+                src_ref=z_in.at[zl], dst_ref=z_in.at[zl], send_sem=send_sem.at[2], recv_sem=recv_sem.at[2],
+                device_id=z_peer(k), device_id_type=MESH,
+            ).start()
+        most = z_in.at[pl.ds(0, 3)]
+        pltpu.make_async_copy(most, most, recv_sem.at[2]).wait()
+
+    @pl.when(jnp.logical_not(owner))
+    def _():
+        pltpu.make_async_copy(z_in, z_in, recv_sem.at[2]).wait()
+
+    gram_ref[mine] = jnp.sum(z_in[...], axis=0)
 
     for step in plane:
         pltpu.make_async_remote_copy(
-            src_ref=gram_ref.at[core, q], dst_ref=gram_ref.at[core, q], send_sem=send_sem.at[4],
-            recv_sem=recv_sem.at[4], device_id=xy_peer(step)[1], device_id_type=MESH,
+            src_ref=gram_ref.at[mine], dst_ref=gram_ref.at[mine], send_sem=send_sem.at[3],
+            recv_sem=recv_sem.at[3], device_id=plane_peer(step)[1], device_id_type=MESH,
         ).start()
-    most = gram_ref.at[core, pl.ds(0, 15)]
-    pltpu.make_async_copy(most, most, recv_sem.at[4]).wait()
-    swap = pltpu.make_async_remote_copy(
-        src_ref=gram_ref.at[core], dst_ref=gram_ref.at[core], send_sem=send_sem.at[5], recv_sem=recv_sem.at[5],
-        device_id=mate, device_id_type=MESH,
-    )
-    swap.start()
-    swap.wait_recv()
+    most = gram_ref.at[pl.ds(0, 31)]
+    pltpu.make_async_copy(most, most, recv_sem.at[3]).wait()
 
     energies = energies_ref[...]
     target = energies - jnp.sum(energies, axis=1, keepdims=True) / SAMPLES
@@ -322,20 +306,23 @@
         result[n : n + 1, :] = full[:, 128 * n : 128 * n + 128]
     result[3:4, :] = full[:, 0:128]
     for step in plane:
-        pltpu.make_async_remote_copy(
-            src_ref=result, dst_ref=results.at[q], send_sem=send_sem.at[6], recv_sem=recv_sem.at[6],
-            device_id=xy_peer(step)[1], device_id_type=MESH,
-        ).start()
+        if step[2] == 0:
+            pltpu.make_async_remote_copy(
+                src_ref=result, dst_ref=results.at[q], send_sem=send_sem.at[4], recv_sem=recv_sem.at[4],
+                device_id=plane_peer(step)[1], device_id_type=MESH,
+            ).start()
     results[q] = result[...]
     most = results.at[pl.ds(0, 15)]
-    pltpu.make_async_copy(most, most, recv_sem.at[6]).wait()
+    pltpu.make_async_copy(most, most, recv_sem.at[4]).wait()
     rest_ref[...] = results[:, 0:2, :]
     update_ref[...] = results[:, 2, :]
 
-    for part, n in (
-        (rbuf.at[pl.ds(0, 31)], 0), (pair_out, 1), (half.at[pl.ds(0, 15)], 2), (z_in.at[pl.ds(0, 7)], 3),
-        (gram_ref.at[0, pl.ds(0, 15)], 4), (gram_ref.at[0], 5), (results.at[pl.ds(0, 15)], 6),
-    ):
+    @pl.when(owner)
+    def _():
+        for part, n in ((plane_in.at[pl.ds(0, 31)], 1), (plane_in.at[pl.ds(0, 7)], 2)):
+            pltpu.make_async_copy(part, part, send_sem.at[n]).wait()
+
+    for part, n in ((rbuf.at[pl.ds(0, 31)], 0), (gram_ref.at[pl.ds(0, 31)], 3), (results.at[pl.ds(0, 15)], 4)):
         pltpu.make_async_copy(part, part, send_sem.at[n]).wait()
 
 
@@ -364,18 +351,16 @@
             pltpu.VMEM((16, 32, 128), BF16),
             pltpu.VMEM((NSAMP, 32, 128), BF16),
             pltpu.VMEM((SAMPLES, 384), BF16),
-            pltpu.VMEM((16, 8, 128), F32),
-            pltpu.VMEM((16, 8, 128), F32),
-            pltpu.VMEM((16, 8, 128), F32),
-            pltpu.VMEM((16, 8, 128), F32),
-            pltpu.VMEM((8, 8, 128), F32),
-            pltpu.VMEM((2, 16, 2, 8, 128), F32),
+            pltpu.VMEM((32, 8, SAMPLES), F32),
+            pltpu.VMEM((32, 8, SAMPLES), F32),
+            pltpu.VMEM((4, 8, SAMPLES), F32),
+            pltpu.VMEM((32, 8, SAMPLES), F32),
             pltpu.VMEM((SAMPLES, SAMPLES), F32),
             pltpu.VMEM((SAMPLES, SAMPLES), F32),
             pltpu.VMEM((4, 128), F32),
             pltpu.VMEM((16, 4, 128), F32),
-            pltpu.SemaphoreType.DMA((7,)),
-            pltpu.SemaphoreType.DMA((7,)),
+            pltpu.SemaphoreType.DMA((5,)),
+            pltpu.SemaphoreType.DMA((5,)),
             pltpu.SemaphoreType.DMA((9,)),
         ],
         compiler_params=pltpu.CompilerParams(

time: 52.8 us -> 49.9 us (0.945)
  Pallas kernels: 49.5 us -> 46.7 us
    pallas_call x1, Pallas kernels: 49.5 us -> 46.7 us  [per_device(): pl.pallas_call(kernel, out_shape=(jax.ShapeDtypeStruct((1, OWN), F32), ja...]
where the time goes in v4:
time: 49.9 us; the launch traced here: 49.8 us
  Pallas kernels  46.7 us (94%)
  local copies, waits for them, and re-layouts  1.79 us (4%)
  between operations  1.29 us (3%)
    pallas_call x1, Pallas kernels, per_device(): pl.pallas_call(kernel, out_shape=(jax.ShapeDtypeStruct((1, OWN), F32), ja...  46.7 us
    unnamed x2, local copies, waits for them, and re-layouts  1.12 us

profile of v4, /device:TPU:1, one launch (start us, length us, event | category | flops | bytes accessed | tf_op | source)
XLA Modules:
  0.0 49.8 jit_solution(11675947780734023321)
XLA Ops:
  1.3 46.7 %update.1 = (f32[1,8]{1,0:T(1,128)S(1)}, f32[16,128]{1,0:T(8,128)S(1)}, f32[16,2,128]{2,1,0:T(2,128)S(1)}) custom-call(s32[8,100]{1,0:T(8,128)} %spins_hbm.1, f32[4,64]{1,0:T(4,128)} %embed_hbm.1, f32[25,64]{1,0:T(8,128)} %position_hbm.1, bf16[32,64]{1,0:T(8,128)(2,1)} %bitcast.12, f32[1,32]{1,0:T(1,128)} %bitcast.14, f32[1,32]{1,0:T(1,128)} %bitcast.15, ...), custom_call_target="tpu_custom_call" | custom-call | tf_op jit(solution)/shard_map/update/pallas_call | solution.py:336
  48.0 0.7 %reshape.32 = f32[32,64]{1,0:T(8,128)} reshape(f32[16,128]{1,0:T(8,128)S(1)} %get-tuple-element.7) | data formatting | bytes 16384 | tf_op jit(solution)/shard_map/reshape | solution.py:371
  48.7 0.5 %copy.15 = f32[8]{0:T(128)} copy(f32[8]{0:T(128)S(1)} %bitcast.10) | data formatting | bytes 64
  49.2 0.6 %copy.16 = f32[4096]{0:T(1024)} copy(f32[4096]{0:T(1024)S(1)} %bitcast.9) | data formatting | bytes 32768

commit v5 on v4

v5 whole, which is shorter than its diff:
```python
import functools
import itertools

import jax
import jax.numpy as jnp
from jax import lax
from jax.experimental import pallas as pl
from jax.experimental.pallas import tpu as pltpu
from jax.sharding import PartitionSpec as P

MESH = pl.DeviceIdType.MESH
HI = lax.Precision.HIGHEST
F32 = jnp.float32
BF16 = jnp.bfloat16

LSIDE = 10
PATCHES = 25
D = 64
SAMPLES = 256
OWN = 8
FOWN = 32
NSAMP = 32
NPAR = 8
NX, NZH, NY = 4, 2, 4
PANEL = 16
ROWS = 512


def place():
    samp = lax.axis_index("samp")
    par = lax.axis_index("par")
    x, zh, y = samp // 8, (samp // 4) % 2, samp % 4
    zl, core = par // 2, par % 2
    return samp, par, x, zh, y, zl, core


def site_patch(site):
    line = (site * 205) >> 11
    at = site - line * 10
    return (line >> 1) * 5 + (at >> 1), (line & 1) * 2 + (at & 1)


def patterns(shape, dim):
    pattern = lax.broadcasted_iota(jnp.int32, shape, dim) & 15
    return [jnp.where((pattern >> k) & 1 == 1, 1.0, -1.0) for k in range(4)]


def tables(q, embed_ref, position_ref, w_ref, bias_ref, readout_ref, table, w_pad, terms, match):
    for half in (0, D):
        table[0:4, half : half + D] = embed_ref[...]
        table[8 : 8 + PATCHES, half : half + D] = position_ref[...]
    hidden = sum(sign * table[k : k + 1, :] for k, sign in enumerate(patterns((ROWS, 128), 0)))
    hidden += jnp.concatenate(
        [jnp.broadcast_to(table[8 + p : 9 + p, :], (16, 128)) for p in range(PATCHES)]
        + [jnp.zeros((ROWS - 16 * PATCHES, 128), F32)], axis=0
    )
    hidden = hidden.astype(BF16)
    w_pad[...] = jnp.zeros_like(w_pad)
    w_pad[:, 0:D] = w_ref[...].astype(F32)
    units = jnp.concatenate(
        [jnp.broadcast_to(w_pad[pl.ds(2 * q + n, 1), :], (D, 128)) for n in range(2)], axis=0
    ).astype(BF16)
    lane = lax.broadcasted_iota(jnp.int32, (1, 128), 1)
    unit = lax.broadcasted_iota(jnp.int32, (1, FOWN), 1)

    def along(ref):
        both = [jnp.sum(jnp.where(unit == 2 * q + n, ref[...], 0.0), axis=1, keepdims=True) for n in range(2)]
        return jnp.where(lane < D, both[0], both[1])

    act = lax.dot_general(hidden, units, (((1,), (1,)), ((), ())), preferred_element_type=F32) + along(bias_ref)
    rest = hidden.astype(F32) * (along(readout_ref) * jnp.tanh(act))
    for n in range(3):
        term = rest.astype(BF16)
        terms[:, 128 * n : 128 * n + 128] = term
        rest = rest - term.astype(F32)
    shape = (128, ROWS)
    patch, place_in = site_patch(lax.broadcasted_iota(jnp.int32, shape, 0))
    signs = patterns(shape, 1)
    sign = jnp.where(
        place_in == 0, signs[0], jnp.where(place_in == 1, signs[1], jnp.where(place_in == 2, signs[2], signs[3]))
    )
    match[...] = jnp.where(patch == lax.broadcasted_iota(jnp.int32, shape, 1) >> 4, sign, 0.0).astype(BF16)


def derivatives(spins_all, terms, match):
    got = spins_all[...].astype(F32)
    spins = jnp.concatenate(
        [
            got[x * 4 + y, 8 * zh : 8 * zh + 8, :]
            for x, zh, y in itertools.product(range(NX), range(NZH), range(NY))
        ], axis=0
    ).astype(BF16)
    score = jnp.dot(spins, match[...], preferred_element_type=F32)
    has = jnp.where(score > 3.5, 1.0, 0.0).astype(BF16)
    grads = jnp.dot(has, terms[...], preferred_element_type=F32)
    return grads[:, 0:128] + (grads[:, 128:256] + grads[:, 256:384])


def offsets(dims):
    def far(step):
        return sum({"zh": 4 * d, "core": 0}.get(name, min(d, 4 - d)) for name, d in zip(dims, step))
    sizes = [4 if name in "xy" else 2 for name in dims]
    return sorted(filter(any, itertools.product(*map(range, sizes))), key=far, reverse=True)


def solve(gram_ref, shift, target, upper_ref, scaled_ref):
    lane = lax.broadcasted_iota(jnp.int32, (8, 128), 1)
    sub = lax.broadcasted_iota(jnp.int32, (8, 128), 0)
    tiles = PANEL // 8
    panels = SAMPLES // PANEL
    corner = jnp.transpose(jnp.concatenate([jnp.zeros((112, 128), F32), gram_ref[14, 0], gram_ref[15, 0]], axis=0))
    reach = {}
    for m in range(panels):
        base = PANEL * m
        diag, off = base // 128, base % 128
        for n in (0, 1) if m == 0 else ((m + 1,) if m + 1 < panels else ()):
            first = PANEL * n
            owed = None
            if m:
                row = lax.broadcasted_iota(jnp.int32, (base, 128), 0)
                col = lax.broadcasted_iota(jnp.int32, (base, 128), 1)
                right = []
                for half in range(2):
                    part = scaled_ref[0:base, 128 * half : 128 * half + 128]
                    if half < diag:
                        part = jnp.where(col + 128 * half <= row, part, 0.0)
                    elif half == diag:
                        part = jnp.where((col >= off) | (col + 128 * half <= row), part, 0.0)
                    right.append(part)
                owed = lax.dot_general(
                    upper_ref[0:base, first : first + PANEL], jnp.concatenate(right, axis=1),
                    (((0,), (0,)), ((), ())), preferred_element_type=F32, precision=HI,
                )
            rows = []
            for tile in range(tiles):
                pair = []
                for half in range(2):
                    if half == 0 and first >= 128:
                        part = jnp.zeros((8, 128), F32) if diag else corner[8 * tile : 8 * tile + 8, :]
                    else:
                        part = gram_ref[first // 8 + tile, 1 - half]
                    at = first + 8 * tile - 128 * half
                    if 0 <= at < 128:
                        part = jnp.where(lane == sub + at, part + shift, part)
                    if half < diag:
                        part = jnp.zeros_like(part)
                    elif half == diag and off:
                        part = jnp.where(lane >= off, part, 0.0)
                    if owed is not None:
                        part = part - owed[8 * tile : 8 * tile + 8, 128 * half : 128 * half + 128]
                    pair.append(part)
                rows.append(pair)
            reach[n] = rows
        near = [n for n in (m, m + 1) if n < panels]
        inside = (lane >= off) & (lane < off + PANEL)
        column = {}
        for j in range(PANEL):
            for n in near:
                for tile in range(tiles):
                    column[j, n, tile] = jnp.broadcast_to(reach[n][tile][diag][:, off + j : off + j + 1], (8, 128))
        for n in near:
            for tile in range(tiles):
                reach[n][tile][diag] = jnp.where(inside, 0.0, reach[n][tile][diag])
        for j in range(PANEL):
            mine, at = j // 8, j % 8
            inverse = 1.0 / column[j, m, mine][at : at + 1, :]
            live = [
                (n, tile) for n in near for tile in range(tiles)
                if n > m or tile > mine or (tile == mine and at < 7)
            ]
            for k in range(j + 1, PANEL):
                factor = column[k, m, mine][at : at + 1, :] * inverse
                for n, tile in live:
                    column[k, n, tile] = column[k, n, tile] - column[j, n, tile] * factor
            for half in range(2):
                pivot_row = reach[m][mine][half][at : at + 1, :]
                if half == diag:
                    pivot_row = jnp.where(lane[0:1] == off + j, 1.0, pivot_row)
                scaled = pivot_row * inverse
                upper_ref[base + j : base + j + 1, 128 * half : 128 * half + 128] = pivot_row
                scaled_ref[base + j : base + j + 1, 128 * half : 128 * half + 128] = scaled
                for n, tile in live:
                    reach[n][tile][half] = reach[n][tile][half] - column[j, n, tile] * scaled
        del reach[m]
    row = lax.broadcasted_iota(jnp.int32, (SAMPLES, SAMPLES), 0)
    col = lax.broadcasted_iota(jnp.int32, (SAMPLES, SAMPLES), 1)
    low = col <= row
    half_solved = jnp.sum(jnp.where(low, upper_ref[...], 0.0) * target, axis=1, keepdims=True)
    return jnp.sum(jnp.where(low, scaled_ref[...], 0.0) * half_solved, axis=0, keepdims=True)


def center(joined):
    mean = jnp.sum(joined, axis=0, keepdims=True) / SAMPLES
    return ((joined - mean) * 0.0625).astype(BF16)


def kernel(
    spins_hbm, embed_hbm, position_hbm, w_hbm, bias_hbm, readout_hbm, other_hbm, energies_hbm, shift_hbm,
    coeffs_ref, update_ref, rest_ref,
    spins_ref, embed_ref, position_ref, w_ref, bias_ref, readout_ref, other_ref, energies_ref, shift_ref,
    spin_pad, table, w_pad, terms, match, spin_tile, spin_mirror, spins_all, sbuf, rbuf, cbuf, gram_part, plane_in, z_in, gram_ref, count_ref,
    upper, scaled, result, results, send_sem, recv_sem, load_sem, ready,
):
    samp, par, x, zh, y, zl, core = place()
    q = x * 4 + y
    z = zh * 4 + zl
    mine = core * 16 + q
    owner = zh == 0

    def samp_peer(step):
        dx, dz, dy = step
        nq = lax.rem(x + dx, 4) * 4 + lax.rem(y + dy, 4)
        return nq, ((nq // 4) * 8 + lax.rem(zh + dz, 2) * 4 + nq % 4, par)

    def plane_peer(step):
        dx, dy, dc = step
        nq, (to, _) = samp_peer((dx, 0, dy))
        nc = lax.rem(core + dc, 2)
        return nc * 16 + nq, (to, zl * 2 + nc)

    def z_peer(k):
        nz = lax.rem(z + k, 8)
        return (x * 8 + (nz // 4) * 4 + y, (nz % 4) * 2 + core)

    summing = (0, 1, 2, 3)
    mirror = (x * 8 + (1 - zh) * 4 + y, par)
    plane = offsets(("x", "y", "core"))
    column = (4, 3, 5, 2, 6, 1, 7)

    def summing_peer(step):
        nq, _ = samp_peer((step[0], 0, step[1]))
        return nq, ((nq // 4) * 8 + nq % 4, par)

    barrier = pltpu.get_barrier_semaphore()

    @pl.when(owner)
    def _():
        for dx, dy, _dc in [step for step in plane if step[2] == 0] + [(0, 0, 0)]:
            _, to = samp_peer((dx, 1, dy))
            pl.semaphore_signal(barrier, inc=1, device_id=to, device_id_type=MESH)
        for k in column[1:]:
            pl.semaphore_signal(barrier, inc=1, device_id=z_peer(k), device_id_type=MESH)

    for step in plane:
        pl.semaphore_signal(barrier, inc=1, device_id=plane_peer(step)[1], device_id_type=MESH)
    loads = [
        pltpu.make_async_copy(a, b, load_sem.at[n])
        for n, (a, b) in enumerate(
            (
                (spins_hbm, spins_ref), (other_hbm, other_ref), (embed_hbm, embed_ref), (position_hbm, position_ref),
                (w_hbm, w_ref), (bias_hbm, bias_ref), (readout_hbm, readout_ref),
                (energies_hbm, energies_ref), (shift_hbm, shift_ref),
            )
        )
    ]
    for load in loads:
        load.start()
    loads[0].wait()
    loads[1].wait()
    spin_pad[...] = jnp.zeros_like(spin_pad)
    spin_pad[:, 0:100] = spins_ref[...].astype(F32)
    spin_tile[...] = jnp.concatenate([spin_pad[...], jnp.zeros((8, 128), F32)], axis=0).astype(BF16)
    for n in range(16):
        sbuf[n] = jnp.concatenate(
            [other_ref[:, 128 * m : 128 * m + 128].astype(F32) for m in (2 * n, 2 * n + 1)], axis=0
        ).astype(BF16)

    @pl.when(owner)
    def _():
        pl.semaphore_wait(barrier, 34)

    @pl.when(jnp.logical_not(owner))
    def _():
        pl.semaphore_wait(barrier, 50)
        for nz in summing:
            to = (x * 8 + (nz // 4) * 4 + y, (nz % 4) * 2 + core)
            pl.semaphore_signal(ready, inc=1, device_id=to, device_id_type=MESH)

    def share(step):
        nq, to = summing_peer(step)
        pltpu.make_async_remote_copy(
            src_ref=sbuf.at[nq], dst_ref=rbuf.at[samp], send_sem=send_sem.at[0], recv_sem=recv_sem.at[0],
            device_id=to, device_id_type=MESH,
        ).start()

    @pl.when(jnp.logical_not(owner))
    def _():
        pltpu.make_async_remote_copy(
            src_ref=spin_tile, dst_ref=spin_mirror, send_sem=send_sem.at[6], recv_sem=recv_sem.at[6],
            device_id=mirror, device_id_type=MESH,
        ).start()

    for step in plane:
        if step[2] == 0:
            share(step)

    @pl.when(jnp.logical_not(owner))
    def _():
        share((0, 0))

    for load in loads[2:]:
        load.wait()

    @pl.when(owner)
    def _():
        tables(q, embed_ref, position_ref, w_ref, bias_ref, readout_ref, table, w_pad, terms, match)
        rbuf[samp] = sbuf[q]
        pltpu.make_async_copy(spin_mirror, spin_mirror, recv_sem.at[6]).wait()
        spins_all[q] = jnp.concatenate([spin_pad[...], spin_mirror[...].astype(F32)[0:8, :]], axis=0).astype(BF16)
        for step in plane:
            if step[2] == 0:
                pltpu.make_async_remote_copy(
                    src_ref=spins_all.at[q], dst_ref=spins_all.at[q], send_sem=send_sem.at[7], recv_sem=recv_sem.at[7],
                    device_id=plane_peer(step)[1], device_id_type=MESH,
                ).start()
        most = spins_all.at[pl.ds(0, 15)]
        pltpu.make_async_copy(most, most, recv_sem.at[7]).wait()
        cbuf[:, 256:384] = center(derivatives(spins_all, terms, match))
        most = rbuf.at[pl.ds(0, NSAMP - 1)]
        pltpu.make_async_copy(most, most, recv_sem.at[0]).wait()
        got = rbuf[...].astype(F32)
        for n in range(2):
            cbuf[:, 128 * n : 128 * n + 128] = center(got[:, 8 * n : 8 * n + 8, :].reshape(SAMPLES, 128))

    tiles_of = (2, 1)

    def by_core(act):
        for c in range(2):
            pl.when(core == c)(functools.partial(act, c))

    def tiles(ref, block, count):
        return ref.at[block, pl.ds(0, count)]

    @pl.when(owner)
    def _():
        product = functools.partial(
            lax.dot_general, dimension_numbers=(((1,), (1,)), ((), ())), preferred_element_type=F32
        )
        gram_part[:, 0] = product(cbuf[...], cbuf[128:256, :]).reshape(32, 8, 128)
        gram_part[0:16, 1] = product(cbuf[0:128, :], cbuf[0:128, :]).reshape(16, 8, 128)

        def reduce_plane(c):
            for step in plane:
                to, device = plane_peer(step)
                count = tiles_of[(c + step[2]) % 2]
                pltpu.make_async_remote_copy(
                    src_ref=tiles(gram_part, to, count), dst_ref=tiles(plane_in, mine, count),
                    send_sem=send_sem.at[1], recv_sem=recv_sem.at[1], device_id=device, device_id_type=MESH,
                ).start()
            count = tiles_of[c]
            plane_in[mine, 0:count] = gram_part[mine, 0:count]
            most = tiles(plane_in, pl.ds(0, 31), count)
            pltpu.make_async_copy(most, most, recv_sem.at[1]).wait()
            z_in[zl, 0:count] = jnp.sum(plane_in[:, 0:count], axis=0)

        by_core(reduce_plane)

        pl.semaphore_wait(ready, 4)

        def reduce_column(c):
            part = tiles(z_in, zl, tiles_of[c])
            for k in column:
                pltpu.make_async_remote_copy(
                    src_ref=part, dst_ref=part, send_sem=send_sem.at[2], recv_sem=recv_sem.at[2],
                    device_id=z_peer(k), device_id_type=MESH,
                ).start()
            most = tiles(z_in, pl.ds(0, 3), tiles_of[c])
            pltpu.make_async_copy(most, most, recv_sem.at[2]).wait()

        by_core(reduce_column)
        pltpu.make_async_remote_copy(
            src_ref=cbuf, dst_ref=cbuf, send_sem=send_sem.at[5], recv_sem=recv_sem.at[5],
            device_id=mirror, device_id_type=MESH,
        ).start()

    @pl.when(jnp.logical_not(owner))
    def _():
        def receive(c):
            every = tiles(z_in, pl.ds(0, 4), tiles_of[c])
            pltpu.make_async_copy(every, every, recv_sem.at[2]).wait()

        by_core(receive)

    def gather_plane(c):
        count = tiles_of[c]
        gram_ref[mine, 0:count] = jnp.sum(z_in[:, 0:count], axis=0)
        part = tiles(gram_ref, mine, count)
        for step in plane:
            pltpu.make_async_remote_copy(
                src_ref=part, dst_ref=part, send_sem=send_sem.at[3], recv_sem=recv_sem.at[3],
                device_id=plane_peer(step)[1], device_id_type=MESH,
            ).start()
        most = count_ref.at[pl.ds(0, 48 - count)]
        pltpu.make_async_copy(most, most, recv_sem.at[3]).wait()

    by_core(gather_plane)

    energies = energies_ref[...]
    target = energies - jnp.sum(energies, axis=1, keepdims=True) / SAMPLES
    x_row = solve(gram_ref, shift_ref[...], target, upper, scaled)
    coeffs_ref[...] = pltpu.roll(
        jnp.broadcast_to(x_row, (8, SAMPLES)), lax.rem(SAMPLES - OWN * samp, SAMPLES), 1
    )[0:1, 0:OWN]

    @pl.when(jnp.logical_not(owner))
    def _():
        pltpu.make_async_copy(cbuf, cbuf, recv_sem.at[5]).wait()

    first = x_row.astype(BF16).astype(F32)
    second = (x_row - first).astype(BF16).astype(F32)
    split = jnp.concatenate([first, second, x_row - first - second, jnp.zeros((13, SAMPLES), F32)], axis=0).astype(BF16)
    full = jnp.dot(split, cbuf[...], preferred_element_type=F32)
    full = full[0:1] + (full[1:2] + full[2:3])
    for n in range(3):
        result[n : n + 1, :] = full[:, 128 * n : 128 * n + 128]
    result[3:4, :] = full[:, 0:128]
    for step in plane:
        if step[2] == 0:
            pltpu.make_async_remote_copy(
                src_ref=result, dst_ref=results.at[q], send_sem=send_sem.at[4], recv_sem=recv_sem.at[4],
                device_id=plane_peer(step)[1], device_id_type=MESH,
            ).start()
    results[q] = result[...]
    most = results.at[pl.ds(0, 15)]
    pltpu.make_async_copy(most, most, recv_sem.at[4]).wait()
    rest_ref[...] = results[:, 0:2, :]
    update_ref[...] = results[:, 2, :]

    def sent(c):
        own = tiles_of[c]
        most = tiles(plane_in, pl.ds(0, 31), own)
        pltpu.make_async_copy(most, most, send_sem.at[3]).wait()

        @pl.when(owner)
        def _():
            for part, n in ((count_ref.at[pl.ds(0, 48 - own)], 1), (tiles(plane_in, pl.ds(0, 7), own), 2)):
                pltpu.make_async_copy(part, part, send_sem.at[n]).wait()

    by_core(sent)

    @pl.when(owner)
    def _():
        for part, n in ((cbuf, 5), (spins_all.at[pl.ds(0, 15)], 7)):
            pltpu.make_async_copy(part, part, send_sem.at[n]).wait()

    @pl.when(jnp.logical_not(owner))
    def _():
        for part, n in ((rbuf.at[0], 0), (spin_tile, 6)):
            pltpu.make_async_copy(part, part, send_sem.at[n]).wait()

    for part, n in ((rbuf.at[pl.ds(0, 15)], 0), (results.at[pl.ds(0, 15)], 4)):
        pltpu.make_async_copy(part, part, send_sem.at[n]).wait()


def per_device(spins, embed, position, w_first, bias_first, readout, other_grads, energies, shift):
    vmem = pl.BlockSpec(memory_space=pltpu.VMEM)
    operands = (
        spins, embed, position, w_first.T, bias_first.reshape(1, -1), readout.reshape(1, -1), other_grads,
        energies.reshape(1, -1), shift.reshape(1, 1),
    )
    operands = tuple(pltpu.with_memory_space_constraint(a, pltpu.HBM) for a in operands[:-1]) + operands[-1:]
    coeffs, update, rest = pl.pallas_call(
        kernel,
        out_shape=(
            jax.ShapeDtypeStruct((1, OWN), F32),
            jax.ShapeDtypeStruct((16, 128), F32),
            jax.ShapeDtypeStruct((16, 2, 128), F32),
        ),
        in_specs=[pl.BlockSpec(memory_space=pltpu.HBM)] * 9,
        out_specs=(vmem,) * 3,
        scratch_shapes=[pltpu.VMEM(a.shape, a.dtype) for a in operands]
        + [
            pltpu.VMEM((8, 128), F32),
            pltpu.VMEM((40, 128), F32),
            pltpu.VMEM((FOWN, 128), F32),
            pltpu.VMEM((ROWS, 384), BF16),
            pltpu.VMEM((128, ROWS), BF16),
            pltpu.VMEM((16, 128), BF16),
            pltpu.VMEM((16, 128), BF16),
            pltpu.VMEM((16, 16, 128), BF16),
            pltpu.VMEM((16, 16, 128), BF16),
            pltpu.VMEM((NSAMP, 16, 128), BF16),
            pltpu.VMEM((SAMPLES, 384), BF16),
            pltpu.VMEM((32, 2, 8, 128), F32),
            pltpu.VMEM((32, 2, 8, 128), F32),
            pltpu.VMEM((4, 2, 8, 128), F32),
            pltpu.VMEM((32, 2, 8, 128), F32),
            pltpu.VMEM((47, 8, 128), F32),
            pltpu.VMEM((SAMPLES, SAMPLES), F32),
            pltpu.VMEM((SAMPLES, SAMPLES), F32),
            pltpu.VMEM((4, 128), F32),
            pltpu.VMEM((16, 4, 128), F32),
            pltpu.SemaphoreType.DMA((8,)),
            pltpu.SemaphoreType.DMA((8,)),
            pltpu.SemaphoreType.DMA((9,)),
            pltpu.SemaphoreType.REGULAR,
        ],
        compiler_params=pltpu.CompilerParams(
            collective_id=0, has_side_effects=True, vmem_limit_bytes=32 * 2**20
        ),
        name="update",
    )(*operands)
    return (coeffs.reshape(-1), update.reshape(FOWN, D).T, rest.reshape(-1))


def solution(mesh):
    return jax.shard_map(
        per_device,
        mesh=mesh,
        in_specs=(
            P("samp", None), P(), P(), P(None, "par"), P("par"), P("par"), P("samp", "par"), P(), P(),
        ),
        out_specs=(P("samp"), P(None, "par"), P("par")),
        check_vma=False,
    )
```

time: 49.9 us -> 49.3 us (0.988)
  Pallas kernels: 46.7 us -> 46.1 us
    pallas_call x1, Pallas kernels: 46.7 us -> 46.1 us  [per_device(): pl.pallas_call(kernel, out_shape=(jax.ShapeDtypeStruct((1, OWN), F32), ja...]
where the time goes in v5:
time: 49.3 us; the launch traced here: 49.2 us
  Pallas kernels  46.1 us (94%)
  local copies, waits for them, and re-layouts  1.79 us (4%)
  between operations  1.29 us (3%)
    pallas_call x1, Pallas kernels, per_device(): pl.pallas_call(kernel, out_shape=(jax.ShapeDtypeStruct((1, OWN), F32), ja...  46.1 us
    unnamed x2, local copies, waits for them, and re-layouts  1.12 us

profile of v5, /device:TPU:1, one launch (start us, length us, event | category | flops | bytes accessed | tf_op | source)
XLA Modules:
  0.0 49.2 jit_solution(9401448761925318872)
XLA Ops:
  1.3 46.1 %update.1 = (f32[1,8]{1,0:T(1,128)S(1)}, f32[16,128]{1,0:T(8,128)S(1)}, f32[16,2,128]{2,1,0:T(2,128)S(1)}) custom-call(s32[8,100]{1,0:T(8,128)} %spins_hbm.1, f32[4,64]{1,0:T(4,128)} %embed_hbm.1, f32[25,64]{1,0:T(8,128)} %position_hbm.1, bf16[32,64]{1,0:T(8,128)(2,1)} %bitcast.12, f32[1,32]{1,0:T(1,128)} %bitcast.14, f32[1,32]{1,0:T(1,128)} %bitcast.15, ...), custom_call_target="tpu_custom_call" | custom-call | tf_op jit(solution)/shard_map/update/pallas_call | solution.py:462
  47.4 0.7 %reshape.32 = f32[32,64]{1,0:T(8,128)} reshape(f32[16,128]{1,0:T(8,128)S(1)} %get-tuple-element.7) | data formatting | bytes 16384 | tf_op jit(solution)/shard_map/reshape | solution.py:503
  48.1 0.5 %copy.15 = f32[8]{0:T(128)} copy(f32[8]{0:T(128)S(1)} %bitcast.10) | data formatting | bytes 64
  48.6 0.6 %copy.16 = f32[4096]{0:T(1024)} copy(f32[4096]{0:T(1024)S(1)} %bitcast.9) | data formatting | bytes 32768

commit v6 on v5

v6 whole, which is shorter than its diff:
```python
import itertools

import jax
import jax.numpy as jnp
from jax import lax
from jax.experimental import pallas as pl
from jax.experimental.pallas import tpu as pltpu
from jax.sharding import PartitionSpec as P

MESH = pl.DeviceIdType.MESH
HI = lax.Precision.HIGHEST
F32 = jnp.float32
BF16 = jnp.bfloat16

LSIDE = 10
PATCHES = 25
D = 64
SAMPLES = 256
OWN = 8
FOWN = 32
NSAMP = 32
NPAR = 8
NX, NZH, NY = 4, 2, 4
PANEL = 16
ROWS = 512


def place():
    samp = lax.axis_index("samp")
    par = lax.axis_index("par")
    x, zh, y = samp // 8, (samp // 4) % 2, samp % 4
    zl, core = par // 2, par % 2
    return samp, par, x, zh, y, zl, core


def site_patch(site):
    line = (site * 205) >> 11
    at = site - line * 10
    return (line >> 1) * 5 + (at >> 1), (line & 1) * 2 + (at & 1)


def patterns(shape, dim):
    pattern = lax.broadcasted_iota(jnp.int32, shape, dim) & 15
    return [jnp.where((pattern >> k) & 1 == 1, 1.0, -1.0) for k in range(4)]


def tables(q, embed_ref, position_ref, weights, table, terms, match):
    for half in (0, D):
        table[0:4, half : half + D] = embed_ref[...]
        table[8 : 8 + PATCHES, half : half + D] = position_ref[...]
    hidden = sum(sign * table[k : k + 1, :] for k, sign in enumerate(patterns((ROWS, 128), 0)))
    hidden += jnp.concatenate(
        [jnp.broadcast_to(table[8 + p : 9 + p, :], (16, 128)) for p in range(PATCHES)]
        + [jnp.zeros((ROWS - 16 * PATCHES, 128), F32)], axis=0
    )
    hidden = hidden.astype(BF16)
    lane = lax.broadcasted_iota(jnp.int32, (1, 128), 1)
    for c in range(2):
        units = jnp.concatenate(
            [jnp.broadcast_to(weights[c, pl.ds(2 * q + n, 1), :], (D, 128)) for n in range(2)], axis=0
        ).astype(BF16)

        def along(row):
            values = weights[c, row : row + 1, :]
            both = [jnp.sum(jnp.where(lane == 2 * q + n, values, 0.0), axis=1, keepdims=True) for n in range(2)]
            return jnp.where(lane < D, both[0], both[1])

        act = lax.dot_general(hidden, units, (((1,), (1,)), ((), ())), preferred_element_type=F32) + along(FOWN)
        rest = hidden.astype(F32) * (along(FOWN + 1) * jnp.tanh(act))
        for n in range(3):
            term = rest.astype(BF16)
            terms[:, 256 * n + 128 * c : 256 * n + 128 * c + 128] = term
            rest = rest - term.astype(F32)
    shape = (128, ROWS)
    patch, place_in = site_patch(lax.broadcasted_iota(jnp.int32, shape, 0))
    signs = patterns(shape, 1)
    sign = jnp.where(
        place_in == 0, signs[0], jnp.where(place_in == 1, signs[1], jnp.where(place_in == 2, signs[2], signs[3]))
    )
    match[...] = jnp.where(patch == lax.broadcasted_iota(jnp.int32, shape, 1) >> 4, sign, 0.0).astype(BF16)


def derivatives(spins_all, terms, match):
    got = spins_all[...].astype(F32)
    spins = jnp.concatenate(
        [
            got[x * 4 + y, 8 * zh : 8 * zh + 8, :]
            for x, zh, y in itertools.product(range(NX), range(NZH), range(NY))
        ], axis=0
    ).astype(BF16)
    score = jnp.dot(spins, match[...], preferred_element_type=F32)
    has = jnp.where(score > 3.5, 1.0, 0.0).astype(BF16)
    grads = jnp.dot(has, terms[...], preferred_element_type=F32)
    return grads[:, 0:256] + (grads[:, 256:512] + grads[:, 512:768])


def offsets():
    def far(step):
        return sum(min(d, 4 - d) for d in step)
    return sorted(filter(any, itertools.product(range(NX), range(NY))), key=far, reverse=True)


def solve(gram_ref, shift, target, upper_ref, scaled_ref):
    lane = lax.broadcasted_iota(jnp.int32, (8, 128), 1)
    sub = lax.broadcasted_iota(jnp.int32, (8, 128), 0)
    tiles = PANEL // 8
    panels = SAMPLES // PANEL
    reach = {}
    for m in range(panels):
        base = PANEL * m
        diag, off = base // 128, base % 128
        for n in (0, 1) if m == 0 else ((m + 1,) if m + 1 < panels else ()):
            first = PANEL * n
            owed = None
            if m:
                row = lax.broadcasted_iota(jnp.int32, (base, 128), 0)
                col = lax.broadcasted_iota(jnp.int32, (base, 128), 1)
                right = []
                for half in range(2):
                    part = scaled_ref[0:base, 128 * half : 128 * half + 128]
                    if half < diag:
                        part = jnp.where(col + 128 * half <= row, part, 0.0)
                    elif half == diag:
                        part = jnp.where((col >= off) | (col + 128 * half <= row), part, 0.0)
                    right.append(part)
                owed = lax.dot_general(
                    upper_ref[0:base, first : first + PANEL], jnp.concatenate(right, axis=1),
                    (((0,), (0,)), ((), ())), preferred_element_type=F32, precision=HI,
                )
            rows = []
            for tile in range(tiles):
                pair = []
                for half in range(2):
                    part = gram_ref[first // PANEL, tile, :, 128 * half : 128 * half + 128]
                    at = first + 8 * tile - 128 * half
                    if 0 <= at < 128:
                        part = jnp.where(lane == sub + at, part + shift, part)
                    if half < diag:
                        part = jnp.zeros_like(part)
                    elif half == diag and off:
                        part = jnp.where(lane >= off, part, 0.0)
                    if owed is not None:
                        part = part - owed[8 * tile : 8 * tile + 8, 128 * half : 128 * half + 128]
                    pair.append(part)
                rows.append(pair)
            reach[n] = rows
        near = [n for n in (m, m + 1) if n < panels]
        inside = (lane >= off) & (lane < off + PANEL)
        column = {}
        for j in range(PANEL):
            for n in near:
                for tile in range(tiles):
                    column[j, n, tile] = jnp.broadcast_to(reach[n][tile][diag][:, off + j : off + j + 1], (8, 128))
        for n in near:
            for tile in range(tiles):
                reach[n][tile][diag] = jnp.where(inside, 0.0, reach[n][tile][diag])
        for j in range(PANEL):
            mine, at = j // 8, j % 8
            inverse = 1.0 / column[j, m, mine][at : at + 1, :]
            live = [
                (n, tile) for n in near for tile in range(tiles)
                if n > m or tile > mine or (tile == mine and at < 7)
            ]
            for k in range(j + 1, PANEL):
                factor = column[k, m, mine][at : at + 1, :] * inverse
                for n, tile in live:
                    column[k, n, tile] = column[k, n, tile] - column[j, n, tile] * factor
            for half in range(2):
                pivot_row = reach[m][mine][half][at : at + 1, :]
                if half == diag:
                    pivot_row = jnp.where(lane[0:1] == off + j, 1.0, pivot_row)
                scaled = pivot_row * inverse
                upper_ref[base + j : base + j + 1, 128 * half : 128 * half + 128] = pivot_row
                scaled_ref[base + j : base + j + 1, 128 * half : 128 * half + 128] = scaled
                for n, tile in live:
                    reach[n][tile][half] = reach[n][tile][half] - column[j, n, tile] * scaled
        del reach[m]
    row = lax.broadcasted_iota(jnp.int32, (SAMPLES, SAMPLES), 0)
    col = lax.broadcasted_iota(jnp.int32, (SAMPLES, SAMPLES), 1)
    low = col <= row
    half_solved = jnp.sum(jnp.where(low, upper_ref[...], 0.0) * target, axis=1, keepdims=True)
    return jnp.sum(jnp.where(low, scaled_ref[...], 0.0) * half_solved, axis=0, keepdims=True)


def center(joined):
    mean = jnp.sum(joined, axis=0, keepdims=True) / SAMPLES
    return ((joined - mean) * 0.0625).astype(BF16)


def kernel(
    spins_hbm, other_hbm, embed_hbm, position_hbm, w_hbm, bias_hbm, readout_hbm, energies_hbm, shift_hbm,
    coeffs_ref, update_ref, rest_ref,
    spins_ref, other_ref, embed_ref, position_ref, w_ref, bias_ref, readout_ref, energies_ref, shift_ref,
    spin_pad, table, weights, terms, match, spin_tile, spin_mirror, spins_all, sbuf, rbuf, cbuf,
    gram_part, plane_in, z_in, gram_ref, upper, scaled, x_buf, result, results, send_sem, recv_sem, load_sem, ready,
):
    samp, par, x, zh, y, zl, core = place()
    q = x * 4 + y
    z = zh * 4 + zl
    lead = core == 1
    follow = jnp.logical_not(lead)
    summing = jnp.logical_and(lead, zh == 0)
    idle = jnp.logical_and(lead, zh == 1)

    def device(nq, nzh, nzl, ncore):
        return ((nq // 4) * 8 + nzh * 4 + nq % 4, nzl * 2 + ncore)

    def beside(step):
        return lax.rem(x + step[0], 4) * 4 + lax.rem(y + step[1], 4)

    def along_z(nz):
        return device(q, nz // 4, nz % 4, 1)

    def send(src, dst, n, to):
        pltpu.make_async_remote_copy(
            src_ref=src, dst_ref=dst, send_sem=send_sem.at[n], recv_sem=recv_sem.at[n], device_id=to, device_id_type=MESH
        ).start()

    def came(part, n):
        pltpu.make_async_copy(part, part, recv_sem.at[n]).wait()

    def left(part, n):
        pltpu.make_async_copy(part, part, send_sem.at[n]).wait()

    plane = offsets()
    mate = device(q, zh, zl, 1 - core)
    mirror = device(q, 1 - zh, zl, 1)

    barrier = pltpu.get_barrier_semaphore()

    def greet(to):
        pl.semaphore_signal(barrier, inc=1, device_id=to, device_id_type=MESH)

    @pl.when(summing)
    def _():
        for step in plane + [(0, 0)]:
            for c in (0, 1):
                greet(device(beside(step), 1, zl, c))
        for k in (3, 5, 2, 6, 1, 7):
            greet(along_z(lax.rem(z + k, 8)))
        for step in plane:
            for c in (0, 1):
                greet(device(beside(step), 0, zl, c))

    @pl.when(idle)
    def _():
        for step in plane:
            greet(device(beside(step), 1, zl, 1))

    greet(mate)

    loads = [
        pltpu.make_async_copy(a, b, load_sem.at[n])
        for n, (a, b) in enumerate(
            (
                (spins_hbm, spins_ref), (other_hbm, other_ref), (embed_hbm, embed_ref), (position_hbm, position_ref),
                (w_hbm, w_ref), (bias_hbm, bias_ref), (readout_hbm, readout_ref),
                (energies_hbm, energies_ref), (shift_hbm, shift_ref),
            )
        )
    ]
    for load in loads:
        load.start()
    for load in loads:
        load.wait()
    spin_pad[...] = jnp.zeros_like(spin_pad)
    spin_pad[:, 0:100] = spins_ref[...].astype(F32)
    spin_tile[...] = jnp.concatenate([spin_pad[...], jnp.zeros((8, 128), F32)], axis=0).astype(BF16)
    for n in range(16):
        sbuf[n] = jnp.concatenate(
            [other_ref[:, 128 * m : 128 * m + 128].astype(F32) for m in (2 * n, 2 * n + 1)], axis=0
        ).astype(BF16)
    weights[core] = jnp.zeros((40, 128), F32)
    weights[core, 0:FOWN, 0:D] = w_ref[...].astype(F32)
    weights[core, FOWN : FOWN + 1, 0:FOWN] = bias_ref[...]
    weights[core, FOWN + 1 : FOWN + 2, 0:FOWN] = readout_ref[...]

    def share(step):
        nq = beside(step)
        send(sbuf.at[nq], rbuf.at[core * NSAMP + samp], 0, device(nq, 0, zl, 1))

    @pl.when(summing)
    def _():
        pl.semaphore_wait(barrier, 19)
        for step in plane:
            share(step)

    @pl.when(idle)
    def _():
        pl.semaphore_wait(barrier, 35)
        send(spin_tile, spin_mirror, 6, mirror)
        for step in plane + [(0, 0)]:
            share(step)
        for nz in range(4):
            pl.semaphore_signal(ready, inc=1, device_id=along_z(nz), device_id_type=MESH)

    @pl.when(jnp.logical_and(follow, zh == 0))
    def _():
        pl.semaphore_wait(barrier, 16)
        for step in plane + [(0, 0)]:
            share(step)
        send(weights.at[0], weights.at[0], 8, mate)

    @pl.when(jnp.logical_and(follow, zh == 1))
    def _():
        pl.semaphore_wait(barrier, 17)
        for step in plane + [(0, 0)]:
            share(step)

    @pl.when(summing)
    def _():
        came(weights.at[0], 8)
        tables(q, embed_ref, position_ref, weights, table, terms, match)
        rbuf[NSAMP + samp] = sbuf[q]
        came(spin_mirror, 6)
        spins_all[q] = jnp.concatenate([spin_pad[...], spin_mirror[...].astype(F32)[0:8, :]], axis=0).astype(BF16)
        for step in plane:
            send(spins_all.at[q], spins_all.at[q], 7, device(beside(step), 0, zl, 1))
        came(spins_all.at[pl.ds(0, 15)], 7)
        cbuf[:, 512:768] = center(derivatives(spins_all, terms, match))
        came(rbuf.at[pl.ds(0, 2 * NSAMP - 1)], 0)
        for c in range(2):
            got = rbuf[NSAMP * c : NSAMP * (c + 1)].astype(F32)
            for n in range(2):
                at = 256 * c + 128 * n
                cbuf[:, at : at + 128] = center(got[:, 8 * n : 8 * n + 8, :].reshape(SAMPLES, 128))

        gram_part[...] = lax.dot_general(
            cbuf[...], cbuf[...], (((1,), (1,)), ((), ())), preferred_element_type=F32
        ).reshape(16, 2, 8, SAMPLES)
        for step in plane:
            nq = beside(step)
            send(gram_part.at[nq], plane_in.at[q], 1, device(nq, 0, zl, 1))
        plane_in[q] = gram_part[q]
        came(plane_in.at[pl.ds(0, 15)], 1)
        z_in[zl] = jnp.sum(plane_in[...], axis=0)

        pl.semaphore_wait(ready, 4)
        for k in (4, 3, 5, 2, 6, 1, 7):
            send(z_in.at[zl], z_in.at[zl], 2, along_z(lax.rem(z + k, 8)))
        came(z_in.at[pl.ds(0, 3)], 2)
        send(cbuf, cbuf, 5, mirror)

    @pl.when(idle)
    def _():
        came(z_in, 2)

    @pl.when(lead)
    def _():
        gram_ref[q] = jnp.sum(z_in[...], axis=0)
        for step in plane:
            send(gram_ref.at[q], gram_ref.at[q], 3, device(beside(step), zh, zl, 1))
        came(gram_ref.at[pl.ds(0, 15)], 3)

        energies = energies_ref[...]
        target = energies - jnp.sum(energies, axis=1, keepdims=True) / SAMPLES
        x_row = solve(gram_ref, shift_ref[...], target, upper, scaled)
        x_buf[...] = jnp.broadcast_to(x_row, (8, SAMPLES))
        send(x_buf, x_buf, 9, mate)

        @pl.when(zh == 1)
        def _():
            came(cbuf, 5)

        first = x_row.astype(BF16).astype(F32)
        second = (x_row - first).astype(BF16).astype(F32)
        split = jnp.concatenate(
            [first, second, x_row - first - second, jnp.zeros((13, SAMPLES), F32)], axis=0
        ).astype(BF16)
        full = jnp.dot(split, cbuf[...], preferred_element_type=F32)
        full = full[0:1] + (full[1:2] + full[2:3])
        result[...] = jnp.zeros_like(result)
        for n, row in enumerate((0, 1, 3, 4, 2, 5)):
            result[row : row + 1, :] = full[:, 128 * n : 128 * n + 128]
        for step in plane:
            send(result, results.at[q], 4, device(beside(step), zh, zl, 1))
        results[q] = result[...]
        came(results.at[pl.ds(0, 15)], 4)
        send(results, results, 10, mate)

    @pl.when(follow)
    def _():
        came(x_buf, 9)
        came(results, 10)

    coeffs_ref[...] = pltpu.roll(x_buf[...], lax.rem(SAMPLES - OWN * samp, SAMPLES), 1)[0:1, 0:OWN]
    for c in range(2):
        @pl.when(core == c)
        def _():
            rest_ref[...] = results[:, 3 * c : 3 * c + 2, :]
            update_ref[...] = results[:, 3 * c + 2, :]

    @pl.when(lead)
    def _():
        for part, n in ((gram_ref.at[pl.ds(0, 15)], 3), (results.at[pl.ds(0, 15)], 4), (x_buf, 9), (results, 10)):
            left(part, n)

    @pl.when(summing)
    def _():
        for part, n in (
            (rbuf.at[pl.ds(0, 15)], 0), (plane_in.at[pl.ds(0, 15)], 1), (plane_in.at[pl.ds(0, 7)], 2), (cbuf, 5),
            (spins_all.at[pl.ds(0, 15)], 7),
        ):
            left(part, n)

    @pl.when(jnp.logical_not(summing))
    def _():
        left(rbuf.at[pl.ds(0, 16)], 0)

    @pl.when(idle)
    def _():
        left(spin_tile, 6)

    @pl.when(jnp.logical_and(follow, zh == 0))
    def _():
        left(weights.at[0], 8)


def per_device(spins, embed, position, w_first, bias_first, readout, other_grads, energies, shift):
    vmem = pl.BlockSpec(memory_space=pltpu.VMEM)
    operands = (
        spins, other_grads, embed, position, w_first.T, bias_first.reshape(1, -1), readout.reshape(1, -1),
        energies.reshape(1, -1), shift.reshape(1, 1),
    )
    operands = tuple(pltpu.with_memory_space_constraint(a, pltpu.HBM) for a in operands[:-1]) + operands[-1:]
    coeffs, update, rest = pl.pallas_call(
        kernel,
        out_shape=(
            jax.ShapeDtypeStruct((1, OWN), F32),
            jax.ShapeDtypeStruct((16, 128), F32),
            jax.ShapeDtypeStruct((16, 2, 128), F32),
        ),
        in_specs=[pl.BlockSpec(memory_space=pltpu.HBM)] * 9,
        out_specs=(vmem,) * 3,
        scratch_shapes=[pltpu.VMEM(a.shape, a.dtype) for a in operands]
        + [
            pltpu.VMEM((8, 128), F32),
            pltpu.VMEM((40, 128), F32),
            pltpu.VMEM((2, 40, 128), F32),
            pltpu.VMEM((ROWS, 768), BF16),
            pltpu.VMEM((128, ROWS), BF16),
            pltpu.VMEM((16, 128), BF16),
            pltpu.VMEM((16, 128), BF16),
            pltpu.VMEM((16, 16, 128), BF16),
            pltpu.VMEM((16, 16, 128), BF16),
            pltpu.VMEM((2 * NSAMP, 16, 128), BF16),
            pltpu.VMEM((SAMPLES, 768), BF16),
            pltpu.VMEM((16, 2, 8, SAMPLES), F32),
            pltpu.VMEM((16, 2, 8, SAMPLES), F32),
            pltpu.VMEM((4, 2, 8, SAMPLES), F32),
            pltpu.VMEM((16, 2, 8, SAMPLES), F32),
            pltpu.VMEM((SAMPLES, SAMPLES), F32),
            pltpu.VMEM((SAMPLES, SAMPLES), F32),
            pltpu.VMEM((8, SAMPLES), F32),
            pltpu.VMEM((8, 128), F32),
            pltpu.VMEM((16, 8, 128), F32),
            pltpu.SemaphoreType.DMA((11,)),
            pltpu.SemaphoreType.DMA((11,)),
            pltpu.SemaphoreType.DMA((9,)),
            pltpu.SemaphoreType.REGULAR,
        ],
        compiler_params=pltpu.CompilerParams(
            collective_id=0, has_side_effects=True, vmem_limit_bytes=32 * 2**20
        ),
        name="update",
    )(*operands)
    return (coeffs.reshape(-1), update.reshape(FOWN, D).T, rest.reshape(-1))


def solution(mesh):
    return jax.shard_map(
        per_device,
        mesh=mesh,
        in_specs=(
            P("samp", None), P(), P(), P(None, "par"), P("par"), P("par"), P("samp", "par"), P(), P(),
        ),
        out_specs=(P("samp"), P(None, "par"), P("par")),
        check_vma=False,
    )
```

time: 49.3 us -> 46 us (0.933)
  Pallas kernels: 46.1 us -> 42.7 us
    pallas_call x1, Pallas kernels: 46.1 us -> 42.7 us  [per_device(): pl.pallas_call(kernel, out_shape=(jax.ShapeDtypeStruct((1, OWN), F32), ja...]
where the time goes in v6:
time: 46 us; the launch traced here: 45.8 us
  Pallas kernels  42.7 us (93%)
  local copies, waits for them, and re-layouts  1.79 us (4%)
  between operations  1.29 us (3%)
    pallas_call x1, Pallas kernels, per_device(): pl.pallas_call(kernel, out_shape=(jax.ShapeDtypeStruct((1, OWN), F32), ja...  42.7 us
    unnamed x2, local copies, waits for them, and re-layouts  1.12 us

profile of v6, /device:TPU:1, one launch (start us, length us, event | category | flops | bytes accessed | tf_op | source)
XLA Modules:
  0.0 45.8 jit_solution(18073102193940616003)
XLA Ops:
  1.3 42.7 %update.1 = (f32[1,8]{1,0:T(1,128)S(1)}, f32[16,128]{1,0:T(8,128)S(1)}, f32[16,2,128]{2,1,0:T(2,128)S(1)}) custom-call(s32[8,100]{1,0:T(8,128)} %spins_hbm.1, bf16[8,4096]{1,0:T(8,128)(2,1)} %other_hbm.1, f32[4,64]{1,0:T(4,128)} %embed_hbm.1, f32[25,64]{1,0:T(8,128)} %position_hbm.1, bf16[32,64]{1,0:T(8,128)(2,1)} %bitcast.12, f32[1,32]{1,0:T(1,128)} %bitcast.14, ...), custom_call_target="tpu_custom_call" | custom-call | tf_op jit(solution)/shard_map/update/pallas_call | solution.py:426
  44.0 0.7 %reshape.32 = f32[32,64]{1,0:T(8,128)} reshape(f32[16,128]{1,0:T(8,128)S(1)} %get-tuple-element.7) | data formatting | bytes 16384 | tf_op jit(solution)/shard_map/reshape | solution.py:467
  44.7 0.5 %copy.15 = f32[8]{0:T(128)} copy(f32[8]{0:T(128)S(1)} %bitcast.10) | data formatting | bytes 64
  45.2 0.6 %copy.16 = f32[4096]{0:T(1024)} copy(f32[4096]{0:T(1024)S(1)} %bitcast.9) | data formatting | bytes 32768

commit v7 on v6

--- a/solution.py
+++ b/solution.py
@@ -247,6 +247,11 @@
         for step in plane:
             greet(device(beside(step), 1, zl, 1))
 
+    @pl.when(follow)
+    def _():
+        for step in plane:
+            greet(device(beside(step), zh, zl, 1))
+
     greet(mate)
 
     loads = [
@@ -281,13 +286,13 @@
 
     @pl.when(summing)
     def _():
-        pl.semaphore_wait(barrier, 19)
+        pl.semaphore_wait(barrier, 34)
         for step in plane:
             share(step)
 
     @pl.when(idle)
     def _():
-        pl.semaphore_wait(barrier, 35)
+        pl.semaphore_wait(barrier, 50)
         send(spin_tile, spin_mirror, 6, mirror)
         for step in plane + [(0, 0)]:
             share(step)
@@ -318,6 +323,11 @@
             send(spins_all.at[q], spins_all.at[q], 7, device(beside(step), 0, zl, 1))
         came(spins_all.at[pl.ds(0, 15)], 7)
         cbuf[:, 512:768] = center(derivatives(spins_all, terms, match))
+
+        def products(columns):
+            return lax.dot_general(columns, columns, (((1,), (1,)), ((), ())), preferred_element_type=F32)
+
+        gram_part[...] = products(cbuf[:, 512:768]).reshape(16, 2, 8, SAMPLES)
         came(rbuf.at[pl.ds(0, 2 * NSAMP - 1)], 0)
         for c in range(2):
             got = rbuf[NSAMP * c : NSAMP * (c + 1)].astype(F32)
@@ -325,9 +335,7 @@
                 at = 256 * c + 128 * n
                 cbuf[:, at : at + 128] = center(got[:, 8 * n : 8 * n + 8, :].reshape(SAMPLES, 128))
 
-        gram_part[...] = lax.dot_general(
-            cbuf[...], cbuf[...], (((1,), (1,)), ((), ())), preferred_element_type=F32
-        ).reshape(16, 2, 8, SAMPLES)
+        gram_part[...] += products(cbuf[:, 0:512]).reshape(16, 2, 8, SAMPLES)
         for step in plane:
             nq = beside(step)
             send(gram_part.at[nq], plane_in.at[q], 1, device(nq, 0, zl, 1))
@@ -350,10 +358,10 @@
         gram_ref[q] = jnp.sum(z_in[...], axis=0)
         for step in plane:
             send(gram_ref.at[q], gram_ref.at[q], 3, device(beside(step), zh, zl, 1))
-        came(gram_ref.at[pl.ds(0, 15)], 3)
-
         energies = energies_ref[...]
         target = energies - jnp.sum(energies, axis=1, keepdims=True) / SAMPLES
+        came(gram_ref.at[pl.ds(0, 15)], 3)
+
         x_row = solve(gram_ref, shift_ref[...], target, upper, scaled)
         x_buf[...] = jnp.broadcast_to(x_row, (8, SAMPLES))
         send(x_buf, x_buf, 9, mate)
@@ -370,29 +378,29 @@
         full = jnp.dot(split, cbuf[...], preferred_element_type=F32)
         full = full[0:1] + (full[1:2] + full[2:3])
         result[...] = jnp.zeros_like(result)
-        for n, row in enumerate((0, 1, 3, 4, 2, 5)):
-            result[row : row + 1, :] = full[:, 128 * n : 128 * n + 128]
-        for step in plane:
-            send(result, results.at[q], 4, device(beside(step), zh, zl, 1))
-        results[q] = result[...]
+        for n, (c, row) in enumerate(((0, 0), (0, 1), (1, 0), (1, 1), (0, 2), (1, 2))):
+            result[c, row : row + 1, :] = full[:, 128 * n : 128 * n + 128]
+        for step in plane:
+            send(result.at[1], results.at[q], 4, device(beside(step), zh, zl, 1))
+        for step in plane + [(0, 0)]:
+            send(result.at[0], results.at[q], 4, device(beside(step), zh, zl, 0))
+        results[q] = result[1]
         came(results.at[pl.ds(0, 15)], 4)
-        send(results, results, 10, mate)
 
     @pl.when(follow)
     def _():
         came(x_buf, 9)
-        came(results, 10)
+        came(results, 4)
 
     coeffs_ref[...] = pltpu.roll(x_buf[...], lax.rem(SAMPLES - OWN * samp, SAMPLES), 1)[0:1, 0:OWN]
-    for c in range(2):
-        @pl.when(core == c)
-        def _():
-            rest_ref[...] = results[:, 3 * c : 3 * c + 2, :]
-            update_ref[...] = results[:, 3 * c + 2, :]
+    rest_ref[...] = results[:, 0:2, :]
+    layer = results[:, 2, :]
+    update_ref[:, 0, :] = layer[:, 0:D]
+    update_ref[:, 1, :] = pltpu.roll(layer, D, 1)[:, 0:D]
 
     @pl.when(lead)
     def _():
-        for part, n in ((gram_ref.at[pl.ds(0, 15)], 3), (results.at[pl.ds(0, 15)], 4), (x_buf, 9), (results, 10)):
+        for part, n in ((gram_ref.at[pl.ds(0, 15)], 3), (results, 4), (results.at[pl.ds(0, 15)], 4), (x_buf, 9)):
             left(part, n)
 
     @pl.when(summing)
@@ -414,6 +422,17 @@
     @pl.when(jnp.logical_and(follow, zh == 0))
     def _():
         left(weights.at[0], 8)
+
+
+def write_out(coeffs, update, rest, coeffs_out, update_out, rest_out, sem):
+    copies = [
+        pltpu.make_async_copy(a, b, sem.at[n])
+        for n, (a, b) in enumerate(((rest, rest_out), (update, update_out), (coeffs, coeffs_out)))
+    ]
+    for copy in copies:
+        copy.start()
+    for copy in copies:
+        copy.wait()
 
 
 def per_device(spins, embed, position, w_first, bias_first, readout, other_grads, energies, shift):
@@ -427,7 +446,7 @@
         kernel,
         out_shape=(
             jax.ShapeDtypeStruct((1, OWN), F32),
-            jax.ShapeDtypeStruct((16, 128), F32),
+            jax.ShapeDtypeStruct((16, 2, D), F32),
             jax.ShapeDtypeStruct((16, 2, 128), F32),
         ),
         in_specs=[pl.BlockSpec(memory_space=pltpu.HBM)] * 9,
@@ -452,10 +471,10 @@
             pltpu.VMEM((SAMPLES, SAMPLES), F32),
             pltpu.VMEM((SAMPLES, SAMPLES), F32),
             pltpu.VMEM((8, SAMPLES), F32),
-            pltpu.VMEM((8, 128), F32),
-            pltpu.VMEM((16, 8, 128), F32),
-            pltpu.SemaphoreType.DMA((11,)),
-            pltpu.SemaphoreType.DMA((11,)),
+            pltpu.VMEM((2, 4, 128), F32),
+            pltpu.VMEM((16, 4, 128), F32),
+            pltpu.SemaphoreType.DMA((10,)),
+            pltpu.SemaphoreType.DMA((10,)),
             pltpu.SemaphoreType.DMA((9,)),
             pltpu.SemaphoreType.REGULAR,
         ],
@@ -464,7 +483,17 @@
         ),
         name="update",
     )(*operands)
-    return (coeffs.reshape(-1), update.reshape(FOWN, D).T, rest.reshape(-1))
+    results = (coeffs, update.reshape(FOWN, D), rest.reshape(NSAMP, 128))
+    results = tuple(pltpu.with_memory_space_constraint(a, pltpu.VMEM) for a in results)
+    coeffs, update, rest = pl.pallas_call(
+        write_out,
+        out_shape=tuple(jax.ShapeDtypeStruct(a.shape, a.dtype) for a in results),
+        in_specs=[vmem] * 3,
+        out_specs=(pl.BlockSpec(memory_space=pltpu.HBM),) * 3,
+        scratch_shapes=[pltpu.SemaphoreType.DMA((3,))],
+        name="write_out",
+    )(*results)
+    return (coeffs.reshape(-1), update.T, rest.reshape(-1))
 
 
 def solution(mesh):

time: 46 us -> 44.2 us (0.961)
  local copies, waits for them, and re-layouts: 1.79 us -> 0 us
    unnamed x2 -> x0, local copies, waits for them, and re-layouts: 1.12 us -> none
    reshape x1 -> x0, local copies, waits for them, and re-layouts: 0.68 us -> none  [per_device(): return (coeffs.reshape(-1), update.reshape(FOWN, D).T, rest.reshape(-1))]
    pallas_call x0 -> x1, Pallas kernels: none -> 0.64 us  [per_device(): pl.pallas_call(write_out, out_shape=tuple((jax.ShapeDtypeStruct(a.shape,...]
    pallas_call x1, Pallas kernels: 42.7 us -> 42.2 us  [per_device(): pl.pallas_call(kernel, out_shape=(jax.ShapeDtypeStruct((1, OWN), F32), ja...]
where the time goes in v7:
time: 44.2 us; the launch traced here: 44.1 us
  Pallas kernels  42.8 us (97%)
  between operations  1.29 us (3%)
    pallas_call x1, Pallas kernels, per_device(): pl.pallas_call(kernel, out_shape=(jax.ShapeDtypeStruct((1, OWN), F32), ja...  42.2 us

profile of v7, /device:TPU:1, one launch (start us, length us, event | category | flops | bytes accessed | tf_op | source)
XLA Modules:
  0.0 44.1 jit_solution(2676985017153566427)
XLA Ops:
  1.3 42.2 %update.1 = (f32[1,8]{1,0:T(1,128)S(1)}, f32[16,2,64]{2,1,0:T(2,128)S(1)}, f32[16,2,128]{2,1,0:T(2,128)S(1)}) custom-call(s32[8,100]{1,0:T(8,128)} %spins_hbm.1, bf16[8,4096]{1,0:T(8,128)(2,1)} %other_hbm.1, f32[4,64]{1,0:T(4,128)} %embed_hbm.1, f32[25,64]{1,0:T(8,128)} %position_hbm.1, bf16[32,64]{1,0:T(8,128)(2,1)} %bitcast.13, f32[1,32]{1,0:T(1,128)} %bitcast.15, ...), custom_call_target="tpu_custom_call" | custom-call | tf_op jit(solution)/shard_map/update/pallas_call | solution.py:445
  43.5 0.6 %write_out.1 = (f32[1,8]{1,0:T(1,128)}, f32[32,64]{1,0:T(8,128)}, f32[32,128]{1,0:T(8,128)}) custom-call(f32[1,8]{1,0:T(1,128)S(1)} %get-tuple-element.9.coeffs, f32[32,64]{1,0:T(8,128)S(1)} %bitcast.11, f32[32,128]{1,0:T(8,128)S(1)} %bitcast.12), custom_call_target="tpu_custom_call" | custom-call | tf_op jit(solution)/shard_map/write_out/pallas_call | solution.py:488

commit v8 on v7

--- a/solution.py
+++ b/solution.py
@@ -100,9 +100,15 @@
     return sorted(filter(any, itertools.product(range(NX), range(NY))), key=far, reverse=True)
 
 
-def solve(gram_ref, shift, target, upper_ref, scaled_ref):
+def solve(gram_ref, shift, target, upper_ref, scaled_ref, upper_terms, scaled_terms):
     lane = lax.broadcasted_iota(jnp.int32, (8, 128), 1)
     sub = lax.broadcasted_iota(jnp.int32, (8, 128), 0)
+    panel_lane = lax.broadcasted_iota(jnp.int32, (PANEL, 128), 1)
+    nothing = jnp.zeros((PANEL, 128), BF16)
+
+    def product(left, right):
+        return lax.dot_general(left, right, (((0,), (0,)), ((), ())), preferred_element_type=F32)
+
     tiles = PANEL // 8
     panels = SAMPLES // PANEL
     reach = {}
@@ -113,19 +119,26 @@
             first = PANEL * n
             owed = None
             if m:
-                row = lax.broadcasted_iota(jnp.int32, (base, 128), 0)
-                col = lax.broadcasted_iota(jnp.int32, (base, 128), 1)
                 right = []
-                for half in range(2):
-                    part = scaled_ref[0:base, 128 * half : 128 * half + 128]
-                    if half < diag:
-                        part = jnp.where(col + 128 * half <= row, part, 0.0)
-                    elif half == diag:
-                        part = jnp.where((col >= off) | (col + 128 * half <= row), part, 0.0)
-                    right.append(part)
-                owed = lax.dot_general(
-                    upper_ref[0:base, first : first + PANEL], jnp.concatenate(right, axis=1),
-                    (((0,), (0,)), ((), ())), preferred_element_type=F32, precision=HI,
+                for term in range(3):
+                    halves = []
+                    for half in range(2):
+                        pieces = []
+                        for p in range(m):
+                            piece = scaled_terms[term, PANEL * p : PANEL * (p + 1), 128 * half : 128 * half + 128]
+                            start = max(0, PANEL * (p + 1) - 128 * half)
+                            end = off if half == diag else 128
+                            if half <= diag and start < end:
+                                piece = jnp.where((panel_lane < start) | (panel_lane >= end), piece, nothing)
+                            pieces.append(piece)
+                        halves.append(jnp.concatenate(pieces, axis=0))
+                    right.append(jnp.concatenate(halves, axis=1))
+                left = [upper_terms[term, 0:base, first : first + PANEL] for term in range(3)]
+                most = product(jnp.concatenate(left, axis=1), right[0])
+                some = product(jnp.concatenate(left[:2], axis=1), right[1])
+                least = product(left[0], right[2])
+                owed = most[0:16] + (
+                    (most[16:32] + some[0:16]) + (some[16:32] + (most[32:48] + least))
                 )
             rows = []
             for tile in range(tiles):
@@ -174,6 +187,12 @@
                 scaled_ref[base + j : base + j + 1, 128 * half : 128 * half + 128] = scaled
                 for n, tile in live:
                     reach[n][tile][half] = reach[n][tile][half] - column[j, n, tile] * scaled
+        for ref, ref_terms in ((upper_ref, upper_terms), (scaled_ref, scaled_terms)):
+            rest = ref[base : base + PANEL, :]
+            for term in range(3):
+                value = rest.astype(BF16)
+                ref_terms[term, base : base + PANEL, :] = value
+                rest = rest - value.astype(F32)
         del reach[m]
     row = lax.broadcasted_iota(jnp.int32, (SAMPLES, SAMPLES), 0)
     col = lax.broadcasted_iota(jnp.int32, (SAMPLES, SAMPLES), 1)
@@ -192,7 +211,7 @@
     coeffs_ref, update_ref, rest_ref,
     spins_ref, other_ref, embed_ref, position_ref, w_ref, bias_ref, readout_ref, energies_ref, shift_ref,
     spin_pad, table, weights, terms, match, spin_tile, spin_mirror, spins_all, sbuf, rbuf, cbuf,
-    gram_part, plane_in, z_in, gram_ref, upper, scaled, x_buf, result, results, send_sem, recv_sem, load_sem, ready,
+    gram_part, plane_in, z_in, gram_ref, upper, scaled, upper_terms, scaled_terms, x_buf, result, results, send_sem, recv_sem, load_sem, ready,
 ):
     samp, par, x, zh, y, zl, core = place()
     q = x * 4 + y
@@ -362,7 +381,7 @@
         target = energies - jnp.sum(energies, axis=1, keepdims=True) / SAMPLES
         came(gram_ref.at[pl.ds(0, 15)], 3)
 
-        x_row = solve(gram_ref, shift_ref[...], target, upper, scaled)
+        x_row = solve(gram_ref, shift_ref[...], target, upper, scaled, upper_terms, scaled_terms)
         x_buf[...] = jnp.broadcast_to(x_row, (8, SAMPLES))
         send(x_buf, x_buf, 9, mate)
 
@@ -470,6 +489,8 @@
             pltpu.VMEM((16, 2, 8, SAMPLES), F32),
             pltpu.VMEM((SAMPLES, SAMPLES), F32),
             pltpu.VMEM((SAMPLES, SAMPLES), F32),
+            pltpu.VMEM((3, SAMPLES, SAMPLES), BF16),
+            pltpu.VMEM((3, SAMPLES, SAMPLES), BF16),
             pltpu.VMEM((8, SAMPLES), F32),
             pltpu.VMEM((2, 4, 128), F32),
             pltpu.VMEM((16, 4, 128), F32),

time: 44.2 us -> 44.2 us (level)
  no operation moved by 1% of the time
where the time goes in v8:
time: 44.2 us; the launch traced here: 44.1 us
  Pallas kernels  42.8 us (97%)
  between operations  1.29 us (3%)
    pallas_call x1, Pallas kernels, per_device(): pl.pallas_call(kernel, out_shape=(jax.ShapeDtypeStruct((1, OWN), F32), ja...  42.1 us

profile of v8, /device:TPU:1, one launch (start us, length us, event | category | flops | bytes accessed | tf_op | source)
XLA Modules:
  0.0 44.1 jit_solution(14646743429194586149)
XLA Ops:
  1.3 42.1 %update.1 = (f32[1,8]{1,0:T(1,128)S(1)}, f32[16,2,64]{2,1,0:T(2,128)S(1)}, f32[16,2,128]{2,1,0:T(2,128)S(1)}) custom-call(s32[8,100]{1,0:T(8,128)} %spins_hbm.1, bf16[8,4096]{1,0:T(8,128)(2,1)} %other_hbm.1, f32[4,64]{1,0:T(4,128)} %embed_hbm.1, f32[25,64]{1,0:T(8,128)} %position_hbm.1, bf16[32,64]{1,0:T(8,128)(2,1)} %bitcast.13, f32[1,32]{1,0:T(1,128)} %bitcast.15, ...), custom_call_target="tpu_custom_call" | custom-call | tf_op jit(solution)/shard_map/update/pallas_call | solution.py:464
  43.4 0.6 %write_out.1 = (f32[1,8]{1,0:T(1,128)}, f32[32,64]{1,0:T(8,128)}, f32[32,128]{1,0:T(8,128)}) custom-call(f32[1,8]{1,0:T(1,128)S(1)} %get-tuple-element.9.coeffs, f32[32,64]{1,0:T(8,128)S(1)} %bitcast.11, f32[32,128]{1,0:T(8,128)S(1)} %bitcast.12), custom_call_target="tpu_custom_call" | custom-call | tf_op jit(solution)/shard_map/write_out/pallas_call | solution.py:509

commit v9 on v8

--- a/solution.py
+++ b/solution.py
@@ -84,8 +84,7 @@
     got = spins_all[...].astype(F32)
     spins = jnp.concatenate(
         [
-            got[x * 4 + y, 8 * zh : 8 * zh + 8, :]
-            for x, zh, y in itertools.product(range(NX), range(NZH), range(NY))
+            got[n, 0:8, :] for n in range(NSAMP)
         ], axis=0
     ).astype(BF16)
     score = jnp.dot(spins, match[...], preferred_element_type=F32)
@@ -210,7 +209,7 @@
     spins_hbm, other_hbm, embed_hbm, position_hbm, w_hbm, bias_hbm, readout_hbm, energies_hbm, shift_hbm,
     coeffs_ref, update_ref, rest_ref,
     spins_ref, other_ref, embed_ref, position_ref, w_ref, bias_ref, readout_ref, energies_ref, shift_ref,
-    spin_pad, table, weights, terms, match, spin_tile, spin_mirror, spins_all, sbuf, rbuf, cbuf,
+    spin_pad, table, weights, terms, match, spin_tile, spins_all, sbuf, rbuf, cbuf,
     gram_part, plane_in, z_in, gram_ref, upper, scaled, upper_terms, scaled_terms, x_buf, result, results, send_sem, recv_sem, load_sem, ready,
 ):
     samp, par, x, zh, y, zl, core = place()
@@ -260,18 +259,7 @@
         for step in plane:
             for c in (0, 1):
                 greet(device(beside(step), 0, zl, c))
-
-    @pl.when(idle)
-    def _():
-        for step in plane:
-            greet(device(beside(step), 1, zl, 1))
-
-    @pl.when(follow)
-    def _():
-        for step in plane:
-            greet(device(beside(step), zh, zl, 1))
-
-    greet(mate)
+        greet(mate)
 
     loads = [
         pltpu.make_async_copy(a, b, load_sem.at[n])
@@ -299,20 +287,23 @@
     weights[core, FOWN : FOWN + 1, 0:FOWN] = bias_ref[...]
     weights[core, FOWN + 1 : FOWN + 2, 0:FOWN] = readout_ref[...]
 
+    def show(step):
+        send(spin_tile, spins_all.at[samp], 7, device(beside(step), 0, zl, 1))
+
     def share(step):
         nq = beside(step)
         send(sbuf.at[nq], rbuf.at[core * NSAMP + samp], 0, device(nq, 0, zl, 1))
 
     @pl.when(summing)
     def _():
-        pl.semaphore_wait(barrier, 34)
+        pl.semaphore_wait(barrier, 18)
         for step in plane:
             share(step)
+            show(step)
 
     @pl.when(idle)
     def _():
-        pl.semaphore_wait(barrier, 50)
-        send(spin_tile, spin_mirror, 6, mirror)
+        pl.semaphore_wait(barrier, 19)
         for step in plane + [(0, 0)]:
             share(step)
         for nz in range(4):
@@ -327,8 +318,9 @@
 
     @pl.when(jnp.logical_and(follow, zh == 1))
     def _():
-        pl.semaphore_wait(barrier, 17)
+        pl.semaphore_wait(barrier, 16)
         for step in plane + [(0, 0)]:
+            show(step)
             share(step)
 
     @pl.when(summing)
@@ -336,11 +328,8 @@
         came(weights.at[0], 8)
         tables(q, embed_ref, position_ref, weights, table, terms, match)
         rbuf[NSAMP + samp] = sbuf[q]
-        came(spin_mirror, 6)
-        spins_all[q] = jnp.concatenate([spin_pad[...], spin_mirror[...].astype(F32)[0:8, :]], axis=0).astype(BF16)
-        for step in plane:
-            send(spins_all.at[q], spins_all.at[q], 7, device(beside(step), 0, zl, 1))
-        came(spins_all.at[pl.ds(0, 15)], 7)
+        spins_all[samp] = spin_tile[...]
+        came(spins_all.at[pl.ds(0, 31)], 7)
         cbuf[:, 512:768] = center(derivatives(spins_all, terms, match))
 
         def products(columns):
@@ -434,9 +423,9 @@
     def _():
         left(rbuf.at[pl.ds(0, 16)], 0)
 
-    @pl.when(idle)
-    def _():
-        left(spin_tile, 6)
+    @pl.when(jnp.logical_and(follow, zh == 1))
+    def _():
+        left(spins_all.at[pl.ds(0, 16)], 7)
 
     @pl.when(jnp.logical_and(follow, zh == 0))
     def _():
@@ -478,8 +467,7 @@
             pltpu.VMEM((ROWS, 768), BF16),
             pltpu.VMEM((128, ROWS), BF16),
             pltpu.VMEM((16, 128), BF16),
-            pltpu.VMEM((16, 128), BF16),
-            pltpu.VMEM((16, 16, 128), BF16),
+            pltpu.VMEM((NSAMP, 16, 128), BF16),
             pltpu.VMEM((16, 16, 128), BF16),
             pltpu.VMEM((2 * NSAMP, 16, 128), BF16),
             pltpu.VMEM((SAMPLES, 768), BF16),

time: 44.2 us -> 44.2 us (level)
  no operation moved by 1% of the time
where the time goes in v9:
time: 44.2 us; the launch traced here: 44.1 us
  Pallas kernels  42.8 us (97%)
  between operations  1.29 us (3%)
    pallas_call x1, Pallas kernels, per_device(): pl.pallas_call(kernel, out_shape=(jax.ShapeDtypeStruct((1, OWN), F32), ja...  42.2 us

profile of v9, /device:TPU:1, one launch (start us, length us, event | category | flops | bytes accessed | tf_op | source)
XLA Modules:
  0.0 44.1 jit_solution(7509495490980348760)
XLA Ops:
  1.3 42.2 %update.1 = (f32[1,8]{1,0:T(1,128)S(1)}, f32[16,2,64]{2,1,0:T(2,128)S(1)}, f32[16,2,128]{2,1,0:T(2,128)S(1)}) custom-call(s32[8,100]{1,0:T(8,128)} %spins_hbm.1, bf16[8,4096]{1,0:T(8,128)(2,1)} %other_hbm.1, f32[4,64]{1,0:T(4,128)} %embed_hbm.1, f32[25,64]{1,0:T(8,128)} %position_hbm.1, bf16[32,64]{1,0:T(8,128)(2,1)} %bitcast.13, f32[1,32]{1,0:T(1,128)} %bitcast.15, ...), custom_call_target="tpu_custom_call" | custom-call | tf_op jit(solution)/shard_map/update/pallas_call | solution.py:453
  43.5 0.6 %write_out.1 = (f32[1,8]{1,0:T(1,128)}, f32[32,64]{1,0:T(8,128)}, f32[32,128]{1,0:T(8,128)}) custom-call(f32[1,8]{1,0:T(1,128)S(1)} %get-tuple-element.9.coeffs, f32[32,64]{1,0:T(8,128)S(1)} %bitcast.11, f32[32,128]{1,0:T(8,128)S(1)} %bitcast.12), custom_call_target="tpu_custom_call" | custom-call | tf_op jit(solution)/shard_map/write_out/pallas_call | solution.py:497
